TPU v7x, 128 devices: a whole 4x4x4 slice. The times are simulated.
128 devices in a mesh: row: 8 (over x, core), col: 16 (over y, z).
Axes of the slice: x: 4, y: 4, z: 4, core: 2. Of those that a mesh axis runs over, the one named last changes fastest.
Arguments:
- x_values: bfloat16 [16, 1048576], P(None, ('row', 'col')), may hold values from -6 to 6
- coords: float32 [3, 1048576], P(None, ('row', 'col')), may hold values from 0 to 1
- weights: float32 [1048576], P(('row', 'col')), may hold values from 0.005 to 0.05
- basis: bfloat16 [4096, 64, 256], P(('row', 'col')), may hold values from -0.375 to 0.375
- transfer: bfloat16 [512, 64, 512], P(('row', 'col')), may hold values from -0.25 to 0.25
- couple0: bfloat16 [4096, 64, 1728], P(('row', 'col')), may hold values from -0.15625 to 0.15625
- couple1: bfloat16 [512, 64, 1728], P(('row', 'col')), may hold values from -0.15625 to 0.15625
- first_far_partner_device: int32 [4096, 27], P(('row', 'col')), may hold values from 0 to 127, all different within a row; in each aligned block of 32 rows (0 to 31, 32 to 63, ...) at most 14 rows name the same one
- far0_box: int32 [4096, 27], P(('row', 'col')), may hold values from 0 to 31
- far1_dev: int32 [512, 27], P(('row', 'col')), may hold values from 0 to 127, all different within a row; in each aligned block of 4 rows (0 to 3, 4 to 7, ...) at most 2 rows name the same one
- far1_box: int32 [512, 27], P(('row', 'col')), may hold values from 0 to 3
- near_partner_device: int32 [4096, 8], P(('row', 'col')), may hold values from 0 to 127, all different within a row; in each aligned block of 32 rows (0 to 31, 32 to 63, ...) at most 4 rows name the same one
- near_box: int32 [4096, 8], P(('row', 'col')), may hold values from 0 to 31
Outputs:
- product: bfloat16 [16, 1048576], P(None, ('row', 'col'))
Inputs may be any that keep to these rules, and one draw needn't show every extreme that they name: `first_far_partner_device`: each row names distinct devices. Among the rows of the leaf boxes of one device, no device is named more than 14 times, and in some device's rows some device is named exactly 14 times. `far1_dev`: each row names distinct devices. Among the rows of the parent boxes of one device, no device is named more than 2 times, and in some device's rows some device is named exactly 2 times. `near_partner_device`: each row names distinct devices. Among the rows of the leaf boxes of one device, no device is named more than 4 times, and in some device's rows some device is named exactly 4 times.
All inputs are finite; a program needn't handle non-finite values.
Results may differ from a plain program's by a relative error of at most 0.0051.
Values may be sent and summed in bfloat16 or wider, within the bound.
No kernel may reach another device: no remote copies, remote signals or barrier semaphores. Data moves between devices by JAX's collectives and lax.ppermute only.
A program may use at most 128 MiB of HBM per device.

v0:
```python
import jax
import jax.numpy as jnp
from jax import lax
from jax.sharding import PartitionSpec as P

wave_number = 20.0
soften = 0.01


def kernel_block(targets, sources, value_entries):
    squared = jnp.zeros(
        targets.shape[:1] + sources.shape[1:2] + (targets.shape[2], sources.shape[3]), jnp.float32
    )
    for coordinate in range(3):
        offset = targets[:, None, coordinate, :, None] - sources[:, :, coordinate, None, :]
        squared = squared + offset * offset
    kernel_evaluator = (
        jnp.cos(wave_number * jnp.sqrt(squared))
        / jnp.sqrt(squared + soften)
        * sources[:, :, 3, None, :]
    )
    return jnp.einsum(
        "qwoj,qwkj->qko",
        kernel_evaluator.astype(jnp.bfloat16),
        value_entries,
        preferred_element_type=jnp.float32,
    )


def grouped(callable_routine, operands, group):
    total = operands[0].shape[0]
    folded = tuple(
        (operand.reshape((total // group, group) + operand.shape[1:]) for operand in operands)
    )
    result = lax.map(lambda member: callable_routine(*member), folded)
    return result.reshape((total,) + result.shape[2:])


def capacity_for(per_device, listed, devices):
    return min(per_device, max(2, (2 * per_device * listed + devices - 1) // devices))


def routing_layout(owners, devices):
    flat_owner = owners.reshape(-1)
    onehot = (flat_owner[:, None] == jnp.arange(devices, dtype=jnp.int32)[None, :]).astype(
        jnp.int32
    )
    before = jnp.cumsum(onehot, axis=0) - onehot
    position = jnp.sum(before * onehot, axis=1)
    return (flat_owner, position)


def request_buffer(flat_owner, position, payload, devices, capacity):
    empty = jnp.zeros((devices, capacity) + payload.shape[1:], payload.dtype)
    return empty.at[flat_owner, position].set(payload)


def plan_requests(coefficients, owners, local_ids, devices):
    capacity = capacity_for(coefficients.shape[0], owners.shape[1], devices)
    flat_owner, position = routing_layout(owners, devices)
    asked = request_buffer(flat_owner, position, local_ids.reshape(-1), devices, capacity)
    return (asked, flat_owner, position)


def fetch_leaf(coefficients, owners, local_ids, devices):
    count, listed = owners.shape
    asked, flat_owner, position = plan_requests(coefficients, owners, local_ids, devices)

    def answer(requested):
        return lax.all_to_all(
            coefficients[requested], ("row", "col"), split_axis=0, concat_axis=0, tiled=True
        )

    replies = answer(lax.all_to_all(asked, ("row", "col"), split_axis=0, concat_axis=0, tiled=True))
    return replies[flat_owner, position].reshape(count, listed, coefficients.shape[1])


def fetch_parent(coefficients, owners, local_ids, devices):
    count, listed = owners.shape
    asked, flat_owner, position = plan_requests(coefficients, owners, local_ids, devices)

    def answer(requested):
        return lax.all_to_all(
            coefficients[requested], ("row", "col"), split_axis=0, concat_axis=0, tiled=True
        )

    replies = answer(lax.all_to_all(asked, ("row", "col"), split_axis=0, concat_axis=0, tiled=True))
    return replies[flat_owner, position].reshape(count, listed, coefficients.shape[1])


def couple_level(wanted, matrices, sides, width):
    count, listed = (wanted.shape[0], wanted.shape[1])
    stacked = (
        wanted.reshape(count, listed, sides, width)
        .transpose(0, 2, 1, 3)
        .reshape(count, sides, listed * width)
    )
    return jnp.einsum("brm,bkm->brk", stacked, matrices, preferred_element_type=jnp.float32)


def near_field(geometry, columns, near_partner_device, near_box, devices):
    boxes, sides, leaf_size = columns.shape
    listed = near_partner_device.shape[1]
    capacity = capacity_for(boxes, listed, devices)
    flat_owner, position = routing_layout(near_partner_device, devices)
    asked = request_buffer(flat_owner, position, near_box.reshape(-1), devices, capacity)

    def answer(requested):
        return (
            lax.all_to_all(
                geometry[requested], ("row", "col"), split_axis=0, concat_axis=0, tiled=True
            ),
            lax.all_to_all(
                columns[requested].astype(jnp.float32),
                ("row", "col"),
                split_axis=0,
                concat_axis=0,
                tiled=True,
            ).astype(jnp.bfloat16),
        )

    got_geometry, got_columns = answer(
        lax.all_to_all(asked, ("row", "col"), split_axis=0, concat_axis=0, tiled=True)
    )
    source_geometry = jnp.concatenate(
        [
            geometry[:, None],
            got_geometry[flat_owner, position].reshape(boxes, listed, 4, leaf_size),
        ],
        1,
    )
    source_columns = jnp.concatenate(
        [
            columns[:, None],
            got_columns[flat_owner, position].reshape(boxes, listed, sides, leaf_size),
        ],
        1,
    )
    return grouped(kernel_block, (geometry[:, :3], source_geometry, source_columns), 4)


def on_device(
    x_values,
    coords,
    weights,
    basis,
    transfer,
    couple0,
    couple1,
    first_far_partner_device,
    far0_box,
    far1_dev,
    far1_box,
    near_partner_device,
    near_box,
):
    devices = lax.axis_size(("row", "col"))
    sides = x_values.shape[0]
    boxes, width, leaf_size = basis.shape
    parent_boxes = transfer.shape[0]
    columns = x_values.reshape(sides, boxes, leaf_size).transpose(1, 0, 2)
    leaf_coef = jnp.einsum(
        "brl,bkl->brk", columns, basis, preferred_element_type=jnp.float32
    ).astype(jnp.bfloat16)
    children = (
        leaf_coef.reshape(parent_boxes, 8, sides, width)
        .transpose(0, 2, 1, 3)
        .reshape(parent_boxes, sides, 8 * width)
    )
    parent_coef = jnp.einsum(
        "prm,pkm->prk", children, transfer, preferred_element_type=jnp.float32
    ).astype(jnp.bfloat16)
    leaf_wanted = fetch_leaf(
        leaf_coef.reshape(boxes, sides * width), first_far_partner_device, far0_box, devices
    )
    leaf_far = couple_level(leaf_wanted, couple0, sides, width)
    parent_wanted = fetch_parent(
        parent_coef.reshape(parent_boxes, sides * width), far1_dev, far1_box, devices
    )
    parent_far = couple_level(parent_wanted, couple1, sides, width)
    spread_across = jnp.einsum(
        "prk,pkm->prm",
        parent_far.astype(jnp.bfloat16),
        transfer,
        preferred_element_type=jnp.float32,
    )
    spread_across = (
        spread_across.reshape(parent_boxes, sides, 8, width)
        .transpose(0, 2, 1, 3)
        .reshape(boxes, sides, width)
    )
    field = (leaf_far + spread_across).astype(jnp.bfloat16)
    far_part = jnp.einsum("brk,bkl->brl", field, basis, preferred_element_type=jnp.float32)
    geometry = (
        jnp.concatenate([coords, weights[None, :]], 0)
        .reshape(4, boxes, leaf_size)
        .transpose(1, 0, 2)
    )
    near_part = near_field(geometry, columns, near_partner_device, near_box, devices)
    total = (far_part + near_part).transpose(1, 0, 2).reshape(sides, boxes * leaf_size)
    return total.astype(jnp.bfloat16)


def solution(mesh):
    placed = (
        P(None, ("row", "col")),
        P(None, ("row", "col")),
        P(("row", "col")),
        P(("row", "col"), None, None),
        P(("row", "col"), None, None),
        P(("row", "col"), None, None),
        P(("row", "col"), None, None),
        P(("row", "col"), None),
        P(("row", "col"), None),
        P(("row", "col"), None),
        P(("row", "col"), None),
        P(("row", "col"), None),
        P(("row", "col"), None),
    )
    return jax.shard_map(
        on_device, mesh=mesh, in_specs=placed, out_specs=P(None, ("row", "col")), check_vma=False
    )
```

profile of v0, /device:TPU:1, one launch (start us, length us, event | category | flops | bytes accessed | tf_op | source)
XLA Modules:
  0.0 624.9 jit_solution(10276306953384746658)
XLA Ops:
  2.9 5.6 scatter_fusion.1
  9.2 11.5 %all-to-all-start.2 = ((s32[128,1,2]{2,1,0:T(1,128)}), s32[128,1,2]{2,1,0:T(1,128)S(1)}, u32[]{:S(2)}, u32[]{:S(2)}) async-start(s32[128,1,2]{2,1,0:T(1,128)} %copy.48), calls=%async_computation.2 | async-start | bytes 131072 | tf_op jit(solution)/shard_map/all_to_all | solution.py:87
  23.9 1.3 convolution_convert_fusion
  27.0 11.1 %scatter_fusion.2 = s32[128,4]{0,1:T(4,128)S(1)} fusion(s32[128,4]{0,1:T(4,128)S(1)} %broadcast.218, s32[256]{0:T(256)S(1)} %bitcast.159, s32[256]{0:T(256)S(1)} %reshape.406), kind=kCustom, calls=%fused_computation.10 | custom fusion | bytes 5120 | tf_op jit(solution)/shard_map/scatter | solution.py:55
  39.1 44.6 %scatter_fusion = s32[128,14]{0,1:T(8,128)S(1)} fusion(s32[128,14]{0,1:T(8,128)S(1)} %broadcast.205, s32[864]{0:T(1024)S(1)} %get-tuple-element.44, s32[864]{0:T(1024)S(1)} %reshape.394), kind=kCustom, calls=%fused_computation.8 | custom fusion | bytes 17280 | tf_op jit(solution)/shard_map/scatter | solution.py:55
  84.5 9.8 %all-to-all-start.4 = ((s32[128,1,4]{2,1,0:T(1,128)}), s32[128,1,4]{2,1,0:T(1,128)S(1)}, u32[]{:S(2)}, u32[]{:S(2)}) async-start(s32[128,1,4]{2,1,0:T(1,128)} %copy.57), calls=%async_computation.4 | async-start | bytes 131072 | tf_op jit(solution)/shard_map/all_to_all | solution.py:123
  94.4 9.3 %all-to-all-done.4 = s32[128,1,4]{2,1,0:T(1,128)S(1)} async-done(((s32[128,1,4]{2,1,0:T(1,128)}), s32[128,1,4]{2,1,0:T(1,128)S(1)}, u32[]{:S(2)}, u32[]{:S(2)}) %all-to-all-start.4) | async-done | bytes 2080 | tf_op jit(solution)/shard_map/all_to_all | solution.py:123
  103.8 4.5 all-to-all-start
  108.3 1.2 gather_fusion.2
  109.4 1.0 reshape.351
  110.4 7.4 %all-to-all-done = s32[128,1,14]{2,1,0:T(1,128)S(1)} async-done(((s32[128,1,14]{2,1,0:T(1,128)}), s32[128,1,14]{2,1,0:T(1,128)S(1)}, u32[]{:S(2)}, u32[]{:S(2)}) %all-to-all-start) | async-done | bytes 7200 | tf_op jit(solution)/shard_map/all_to_all | solution.py:74
  117.9 4.5 all-to-all-start.3
  122.6 3.3 gather_fusion.6
  125.9 10.4 %all-to-all-done.3 = bf16[128,2,1024]{2,1,0:T(2,128)(2,1)S(1)} async-done(((bf16[128,2,1024]{2,1,0:T(2,128)(2,1)}), bf16[128,2,1024]{2,1,0:T(2,128)(2,1)S(1)}, u32[]{:S(2)}, u32[]{:S(2)}) %all-to-all-start.3) | async-done | bytes 524320 | tf_op jit(solution)/shard_map/all_to_all | solution.py:83
  136.2 5.3 all-to-all-start.6
  141.9 6.6 %gather_fusion = bf16[1792,1024]{1,0:T(8,128)(2,1)} fusion(bf16[32,1024]{1,0:T(8,128)(2,1)S(1)} %reshape.316, s32[2048]{0:T(1024)S(1)} %pad_clamp_fusion), kind=kCustom, calls=%fused_computation | custom fusion | bytes 7347200 | tf_op jit(solution)/shard_map/gather | solution.py:71
  148.4 6.4 %reshape.337 = bf16[128,14,1024]{2,1,0:T(8,128)(2,1)} reshape(bf16[1792,1024]{1,0:T(8,128)(2,1)} %gather_fusion) | data formatting | bytes 7340032 | tf_op jit(solution)/shard_map/gather | solution.py:71
  154.8 16.0 %all-to-all-done.6 = f32[128,4,4,256]{3,2,1,0:T(4,128)} async-done(((f32[128,4,4,256]{3,2,1,0:T(4,128)}), f32[128,4,4,256]{3,2,1,0:T(4,128)}, u32[]{:S(2)}, u32[]{:S(2)}) %all-to-all-start.6) | async-done | bytes 2097184 | tf_op jit(solution)/shard_map/all_to_all | solution.py:110
  170.8 6.3 %all-to-all-start.1 = ((bf16[128,14,1024]{2,1,0:T(8,128)(2,1)}), bf16[128,14,1024]{2,1,0:T(8,128)(2,1)}, u32[]{:S(2)}, u32[]{:S(2)}) async-start(bf16[128,14,1024]{2,1,0:T(8,128)(2,1)} %reshape.337), calls=%async_computation.1 | async-start | bytes 8388608 | tf_op jit(solution)/shard_map/all_to_all | solution.py:70
  177.1 3.4 gather_fusion.4
  180.6 48.6 %all-to-all-done.1 = bf16[128,14,1024]{2,1,0:T(8,128)(2,1)} async-done(((bf16[128,14,1024]{2,1,0:T(8,128)(2,1)}), bf16[128,14,1024]{2,1,0:T(8,128)(2,1)}, u32[]{:S(2)}, u32[]{:S(2)}) %all-to-all-start.1) | async-done | bytes 3670048 | tf_op jit(solution)/shard_map/all_to_all | solution.py:70
  229.2 5.9 all-to-all-start.5
  235.4 1.7 gather_fusion.3
  237.9 1.7 fusion.11
  240.4 3.2 gather_fusion.7
  243.8 1.6 pad_maximum_fusion.1
  245.5 6.0 copy.45
  251.5 19.2 %gather_fusion.1 = bf16[864,1024]{1,0:T(8,128)(2,1)S(1)} fusion(bf16[128,14,1024]{2,0,1:T(8,128)(2,1)} %copy.45, s32[864]{0:T(1024)S(1)} %get-tuple-element.43), kind=kCustom, calls=%fused_computation.1 | custom fusion | bytes 3545856 | tf_op jit(solution)/shard_map/gather | solution.py:75
  270.7 3.6 reshape_reshape.6
  274.3 5.1 copy.80
  279.3 15.0 %reshape.321 = bf16[32,16,1728]{2,1,0:T(8,128)(2,1)} reshape(bf16[32,16,27,64]{3,2,1,0:T(8,128)(2,1)} %bitcast.161) | data formatting | bytes 3538944 | tf_op jit(solution)/shard_map/reshape | solution.py:96
  294.4 3.3 gather_fusion.5
  297.7 1.6 pad_maximum_fusion
  299.4 319.3 %while.10 = (s32[]{:T(128)}, f32[8,4,16,256]{3,2,1,0:T(8,128)}, bf16[8,4,9,16,256]{4,3,2,1,0:T(8,128)(2,1)}, f32[8,4,3,256]{3,1,2,0:T(4,128)S(1)}, f32[8,4,9,4,256]{4,2,1,0,3:T(8,128)}, /*index=5*/s32[]{:T(128)}) while((s32[]{:T(128)}, f32[8,4,16,256]{3,2,1,0:T(8,128)}, bf16[8,4,9,16,256]{4,3,2,1,0:T(8,128)(2,1)}, ...), condition=%wide.region_12.13_spmd, body=%wide.region_11.12_spmd.sunk | while | flops 106168320 | bytes 1749085 | solution.py:35
  299.4 1.1 dynamic-slice_bitcast_fusion.4
  300.5 1.0 fusion.51
  301.5 37.9 %fusion.52 = f32[8,4,16,256]{3,2,1,0:T(8,128)} fusion(f32[8,4,16,256]{3,2,1,0:T(8,128)} %get-tuple-element.120, s32[]{:T(128)S(6)} %copy.87, f32[4,9,256]{2,1,0:T(8,128)S(1)} %get-tuple-element.106, f32[4,9,256]{2,1,0:T(8,128)S(1)} %get-tuple-element.107, f32[4,256]{1,0:T(4,128)S(1)} %get-tuple-element.108, ...), kind=kOutput, calls=%fused_computation.14.clone.3 | convolution fusion | flops 106168320 | bytes 520196 | tf_op jit(solution)/shard_map/while/body/eval_jaxpr/qwoj,qwkj->qko/dot_general | solution.py:22
  340.4 1.0 fusion.51
  341.4 37.9 %fusion.52 = f32[8,4,16,256]{3,2,1,0:T(8,128)} fusion(f32[8,4,16,256]{3,2,1,0:T(8,128)} %get-tuple-element.120, s32[]{:T(128)S(6)} %copy.87, f32[4,9,256]{2,1,0:T(8,128)S(1)} %get-tuple-element.106, f32[4,9,256]{2,1,0:T(8,128)S(1)} %get-tuple-element.107, f32[4,256]{1,0:T(4,128)S(1)} %get-tuple-element.108, ...), kind=kOutput, calls=%fused_computation.14.clone.3 | convolution fusion | flops 106168320 | bytes 520196 | tf_op jit(solution)/shard_map/while/body/eval_jaxpr/qwoj,qwkj->qko/dot_general | solution.py:22
  380.3 1.0 fusion.51
  381.3 37.9 %fusion.52 = f32[8,4,16,256]{3,2,1,0:T(8,128)} fusion(f32[8,4,16,256]{3,2,1,0:T(8,128)} %get-tuple-element.120, s32[]{:T(128)S(6)} %copy.87, f32[4,9,256]{2,1,0:T(8,128)S(1)} %get-tuple-element.106, f32[4,9,256]{2,1,0:T(8,128)S(1)} %get-tuple-element.107, f32[4,256]{1,0:T(4,128)S(1)} %get-tuple-element.108, ...), kind=kOutput, calls=%fused_computation.14.clone.3 | convolution fusion | flops 106168320 | bytes 520196 | tf_op jit(solution)/shard_map/while/body/eval_jaxpr/qwoj,qwkj->qko/dot_general | solution.py:22
  421.2 37.9 %fusion.52 = f32[8,4,16,256]{3,2,1,0:T(8,128)} fusion(f32[8,4,16,256]{3,2,1,0:T(8,128)} %get-tuple-element.120, s32[]{:T(128)S(6)} %copy.87, f32[4,9,256]{2,1,0:T(8,128)S(1)} %get-tuple-element.106, f32[4,9,256]{2,1,0:T(8,128)S(1)} %get-tuple-element.107, f32[4,256]{1,0:T(4,128)S(1)} %get-tuple-element.108, ...), kind=kOutput, calls=%fused_computation.14.clone.3 | convolution fusion | flops 106168320 | bytes 520196 | tf_op jit(solution)/shard_map/while/body/eval_jaxpr/qwoj,qwkj->qko/dot_general | solution.py:22
  461.1 37.9 %fusion.52 = f32[8,4,16,256]{3,2,1,0:T(8,128)} fusion(f32[8,4,16,256]{3,2,1,0:T(8,128)} %get-tuple-element.120, s32[]{:T(128)S(6)} %copy.87, f32[4,9,256]{2,1,0:T(8,128)S(1)} %get-tuple-element.106, f32[4,9,256]{2,1,0:T(8,128)S(1)} %get-tuple-element.107, f32[4,256]{1,0:T(4,128)S(1)} %get-tuple-element.108, ...), kind=kOutput, calls=%fused_computation.14.clone.3 | convolution fusion | flops 106168320 | bytes 520196 | tf_op jit(solution)/shard_map/while/body/eval_jaxpr/qwoj,qwkj->qko/dot_general | solution.py:22
  501.0 37.9 %fusion.52 = f32[8,4,16,256]{3,2,1,0:T(8,128)} fusion(f32[8,4,16,256]{3,2,1,0:T(8,128)} %get-tuple-element.120, s32[]{:T(128)S(6)} %copy.87, f32[4,9,256]{2,1,0:T(8,128)S(1)} %get-tuple-element.106, f32[4,9,256]{2,1,0:T(8,128)S(1)} %get-tuple-element.107, f32[4,256]{1,0:T(4,128)S(1)} %get-tuple-element.108, ...), kind=kOutput, calls=%fused_computation.14.clone.3 | convolution fusion | flops 106168320 | bytes 520196 | tf_op jit(solution)/shard_map/while/body/eval_jaxpr/qwoj,qwkj->qko/dot_general | solution.py:22
  539.9 1.0 fusion.51
  540.9 37.9 %fusion.52 = f32[8,4,16,256]{3,2,1,0:T(8,128)} fusion(f32[8,4,16,256]{3,2,1,0:T(8,128)} %get-tuple-element.120, s32[]{:T(128)S(6)} %copy.87, f32[4,9,256]{2,1,0:T(8,128)S(1)} %get-tuple-element.106, f32[4,9,256]{2,1,0:T(8,128)S(1)} %get-tuple-element.107, f32[4,256]{1,0:T(4,128)S(1)} %get-tuple-element.108, ...), kind=kOutput, calls=%fused_computation.14.clone.3 | convolution fusion | flops 106168320 | bytes 520196 | tf_op jit(solution)/shard_map/while/body/eval_jaxpr/qwoj,qwkj->qko/dot_general | solution.py:22
  580.8 37.9 %fusion.52 = f32[8,4,16,256]{3,2,1,0:T(8,128)} fusion(f32[8,4,16,256]{3,2,1,0:T(8,128)} %get-tuple-element.120, s32[]{:T(128)S(6)} %copy.87, f32[4,9,256]{2,1,0:T(8,128)S(1)} %get-tuple-element.106, f32[4,9,256]{2,1,0:T(8,128)S(1)} %get-tuple-element.107, f32[4,256]{1,0:T(4,128)S(1)} %get-tuple-element.108, ...), kind=kOutput, calls=%fused_computation.14.clone.3 | convolution fusion | flops 106168320 | bytes 520196 | tf_op jit(solution)/shard_map/while/body/eval_jaxpr/qwoj,qwkj->qko/dot_general | solution.py:22
  618.7 5.3 fusion.9
  (123 shorter events, 24.6 us)
Async XLA Ops:
  0.0 23.8 %copy-start = (bf16[32,64,256]{2,1,0:T(8,128)(2,1)S(1)}, bf16[32,64,256]{2,1,0:T(8,128)(2,1)}, u32[]{:S(2)}) copy-start(bf16[32,64,256]{2,1,0:T(8,128)(2,1)} %param.18) | copy-start | bytes 3145732
  2.8 23.8 %copy-start.4 = (bf16[4,64,512]{2,1,0:T(8,128)(2,1)S(1)}, bf16[4,64,512]{2,1,0:T(8,128)(2,1)}, u32[]{:S(2)}) copy-start(bf16[4,64,512]{2,1,0:T(8,128)(2,1)} %param.19) | copy-start | bytes 786436
  2.8 24.0 %copy-start.8 = (s32[32,8]{0,1:T(8,128)S(1)}, s32[32,8]{0,1:T(8,128)}, u32[]{:S(2)}) copy-start(s32[32,8]{0,1:T(8,128)} %param.27) | copy-start | bytes 3076
  9.2 75.2 %all-to-all-start.2 = ((s32[128,1,2]{2,1,0:T(1,128)}), s32[128,1,2]{2,1,0:T(1,128)S(1)}, u32[]{:S(2)}, u32[]{:S(2)}) async-start(s32[128,1,2]{2,1,0:T(1,128)} %copy.48), calls=%async_computation.2 | async-start | bytes 131072 | tf_op jit(solution)/shard_map/all_to_all | solution.py:87
  23.8 15.1 %copy-start.7 = (s32[32,27]{1,0:T(8,128)S(1)}, s32[32,27]{1,0:T(8,128)}, u32[]{:S(2)}) copy-start(s32[32,27]{1,0:T(8,128)} %param.23) | copy-start | bytes 10372
  83.7 38.6 %copy-start.5 = (f32[3,8192]{1,0:T(4,128)S(1)}, f32[3,8192]{1,0:T(4,128)}, u32[]{:S(2)}) copy-start(f32[3,8192]{1,0:T(4,128)} %param.16) | copy-start | bytes 294916
  83.7 38.6 %copy-start.6 = (f32[8192]{0:T(1024)S(1)}, f32[8192]{0:T(1024)}, u32[]{:S(2)}) copy-start(f32[8192]{0:T(1024)} %param.17) | copy-start | bytes 98308
  84.5 19.3 %all-to-all-start.4 = ((s32[128,1,4]{2,1,0:T(1,128)}), s32[128,1,4]{2,1,0:T(1,128)S(1)}, u32[]{:S(2)}, u32[]{:S(2)}) async-start(s32[128,1,4]{2,1,0:T(1,128)} %copy.57), calls=%async_computation.4 | async-start | bytes 131072 | tf_op jit(solution)/shard_map/all_to_all | solution.py:123
  103.8 14.1 %all-to-all-start = ((s32[128,1,14]{2,1,0:T(1,128)}), s32[128,1,14]{2,1,0:T(1,128)S(1)}, u32[]{:S(2)}, u32[]{:S(2)}) async-start(s32[128,1,14]{2,1,0:T(1,128)} %copy.44), calls=%async_computation | async-start | bytes 131072 | tf_op jit(solution)/shard_map/all_to_all | solution.py:74
  117.9 18.4 %all-to-all-start.3 = ((bf16[128,2,1024]{2,1,0:T(2,128)(2,1)}), bf16[128,2,1024]{2,1,0:T(2,128)(2,1)S(1)}, u32[]{:S(2)}, u32[]{:S(2)}) async-start(bf16[128,2,1024]{2,1,0:T(2,128)(2,1)} %reshape.351), calls=%async_computation.3 | async-start | bytes 1048576 | tf_op jit(solution)/shard_map/all_to_all | solution.py:83
  136.2 34.6 %all-to-all-start.6 = ((f32[128,4,4,256]{3,2,1,0:T(4,128)}), f32[128,4,4,256]{3,2,1,0:T(4,128)}, u32[]{:S(2)}, u32[]{:S(2)}) async-start(f32[128,4,4,256]{3,2,1,0:T(4,128)} %bitcast.162), calls=%async_computation.6 | async-start | bytes 4194304 | tf_op jit(solution)/shard_map/all_to_all | solution.py:110
  154.8 22.3 %copy-start.3 = (bf16[16,8192]{1,0:T(8,128)(2,1)S(1)}, bf16[16,8192]{1,0:T(8,128)(2,1)}, u32[]{:S(2)}) copy-start(bf16[16,8192]{1,0:T(8,128)(2,1)} %param.15) | copy-start | bytes 786436
  170.8 58.3 %all-to-all-start.1 = ((bf16[128,14,1024]{2,1,0:T(8,128)(2,1)}), bf16[128,14,1024]{2,1,0:T(8,128)(2,1)}, u32[]{:S(2)}, u32[]{:S(2)}) async-start(bf16[128,14,1024]{2,1,0:T(8,128)(2,1)} %reshape.337), calls=%async_computation.1 | async-start | bytes 8388608 | tf_op jit(solution)/shard_map/all_to_all | solution.py:70
  229.2 65.2 %all-to-all-start.5 = ((bf16[128,4,16,256]{3,2,1,0:T(8,128)(2,1)}), bf16[128,4,16,256]{3,2,1,0:T(8,128)(2,1)}, u32[]{:S(2)}, u32[]{:S(2)}) async-start(bf16[128,4,16,256]{3,2,1,0:T(8,128)(2,1)} %bitcast.160), calls=%async_computation.5 | async-start | bytes 8388608 | tf_op jit(solution)/shard_map/all_to_all | solution.py:113
  299.4 319.3 %copy-start.1 = (bf16[32,16,1728]{2,1,0:T(8,128)(2,1)S(1)}, bf16[32,16,1728]{2,1,0:T(8,128)(2,1)}, u32[]{:S(2)}) copy-start(bf16[32,16,1728]{2,1,0:T(8,128)(2,1)} %reshape.321) | copy-start | bytes 5308420
  299.4 319.3 %copy-start.2 = (f32[4,16,8,64]{3,1,2,0:T(8,128)S(1)}, f32[4,16,8,64]{3,1,2,0:T(8,128)}, u32[]{:S(2)}) copy-start(f32[4,16,8,64]{3,1,2,0:T(8,128)} %copy.50) | copy-start | bytes 393220
where the time goes:
time: 636 us; the launch traced here: 625 us
  matrix products  311 us (49%)
  local copies, waits for them, and re-layouts  168 us (26%)
  waiting for transfers between devices  91.7 us (14%)
  starting transfers between devices  47.7 us (8%)
    dot_general x8, matrix products, kernel_block(): jnp.einsum('qwoj,qwkj->qko', kernel_evaluator.astype(jnp.bfloat16), value...  303 us
    scatter x3, local copies, waits for them, and re-layouts, request_buffer(): return empty.at[flat_owner, position].set(payload)  61.3 us
    all_to_all x2, waiting for transfers between devices, answer(): lax.all_to_all(coefficients[requested], ('row', 'col'), split_axis=0, con...  58.9 us
    gather x1, local copies, waits for them, and re-layouts, fetch_leaf(): replies[flat_owner, position].reshape(count, listed, coefficients.shape[1])  19.2 us
    all_to_all x1, waiting for transfers between devices, answer(): lax.all_to_all(geometry[requested], ('row', 'col'), split_axis=0, concat_...  16 us
    reshape x2, local copies, waits for them, and re-layouts, couple_level(): stacked = wanted.reshape(count, listed, sides, width).transpose(0, 2, 1,...  15.4 us
    gather x4, local copies, waits for them, and re-layouts, answer(): coefficients[requested]  15.1 us
  transfers between devices with their start and end apart: 7, of which 5 were waited for; matrix products, arithmetic and copies ran while one was open for 23% of the time, Pallas kernels for 0%

commit v1 on v0

v1 whole, which is shorter than its diff:
```python
import functools
import math

import jax
import jax.numpy as jnp
import numpy as np
from jax import lax
from jax.experimental import pallas as pl
from jax.experimental.pallas import tpu as pltpu
from jax.sharding import PartitionSpec as P

AXES = ("row", "col")
LEAF = 256
HALF = 128
WIDTH = 64
SIDES = 16
SLOTS = 4
PART = 2
ROWS = 40 * PART
FEATURES = 48
GROUP = 8
CODE = 248.0
CYCLES = 20.0 / (2.0 * math.pi)
SOFTEN = 0.01 * CYCLES * CYCLES
MAGIC = 12582912.0


def cosine_polynomial(degree):
    nodes = np.cos((np.arange(400) + 0.5) * np.pi / 400) * 0.125 + 0.125
    fit = np.polynomial.chebyshev.Chebyshev.interpolate(
        lambda z: np.cos(2 * np.pi * np.sqrt(np.maximum(z, 0.0))), degree, [0.0, 0.25]
    )
    del nodes
    return [float(c) for c in fit.convert(kind=np.polynomial.Polynomial).coef]


COSINE = cosine_polynomial(4)
LEAD = COSINE[-1]
MONIC = [c / LEAD for c in COSINE[:-1]]
FOLD = LEAD * CYCLES


def split(value):
    high = value.astype(jnp.bfloat16).astype(jnp.float32)
    low = (value - high).astype(jnp.bfloat16).astype(jnp.float32)
    return high, low


def contract_last(a, b):
    return lax.dot_general(a, b, (((1,), (1,)), ((), ())), preferred_element_type=jnp.float32)


def vmem():
    return pl.BlockSpec(memory_space=pltpu.VMEM)


def smem():
    return pl.BlockSpec(memory_space=pltpu.SMEM)


def coef_kernel(x_ref, basis_ref, transfer_ref, out_ref):
    boxes = basis_ref.shape[0]
    parents = transfer_ref.shape[0]
    leaf = []
    for b in range(boxes):
        c = contract_last(x_ref[:, b * LEAF : (b + 1) * LEAF], basis_ref[b])
        leaf.append(c)
        if b % 2:
            out_ref[b // 2] = jnp.concatenate([leaf[b - 1], c], axis=1).astype(jnp.bfloat16)
    up = []
    for p in range(parents):
        children = jnp.concatenate([out_ref[4 * p + i] for i in range(4)], axis=1)
        up.append(contract_last(children, transfer_ref[p]))
        if p % 2:
            out_ref[boxes // 2 + p // 2] = jnp.concatenate([up[p - 1], up[p]], axis=1).astype(
                jnp.bfloat16
            )


def plan_kernel(dev_ref, box_ref, asked_ref, place_ref):
    count, listed = dev_ref.shape
    devices = asked_ref.shape[0]
    lane = lax.broadcasted_iota(jnp.int32, (count, devices), 1)
    dev, box = dev_ref[...], box_ref[...]
    named = jnp.zeros((count, devices), jnp.float32)
    wanted = jnp.zeros((count, devices), jnp.float32)
    hits = []
    for i in range(listed):
        hit = (dev[:, i : i + 1] == lane).astype(jnp.float32)
        hits.append(hit)
        named = named + hit
        wanted = wanted + hit * box[:, i : i + 1].astype(jnp.float32)
    row = lax.broadcasted_iota(jnp.int32, (count, count), 0)
    col = lax.broadcasted_iota(jnp.int32, (count, count), 1)
    before = jnp.dot(
        (col < row).astype(jnp.bfloat16),
        named.astype(jnp.bfloat16),
        preferred_element_type=jnp.float32,
    )
    slot = lax.broadcasted_iota(jnp.int32, (devices, devices), 0)
    asked = jnp.zeros((devices, devices), jnp.float32)
    for p in range(SLOTS):
        here = jnp.sum(
            jnp.where((before == p) & (named > 0), wanted, 0.0), axis=0, keepdims=True
        )
        asked = jnp.where(slot == p, here, asked)
    asked_ref[...] = asked.T.astype(jnp.int32)
    column = lax.broadcasted_iota(jnp.int32, (count, listed), 1)
    position = jnp.zeros((count, listed), jnp.float32)
    for i in range(listed):
        at = jnp.sum(hits[i] * before, axis=1, keepdims=True)
        position = jnp.where(column == i, at, position)
    place_ref[...] = dev * SLOTS + position.astype(jnp.int32)


def prepare_kernel(x_ref, weight_ref, source_ref, target_ref, table_ref, feature_ref):
    boxes = target_ref.shape[0]
    for b in range(boxes):
        for h in range(2):
            at = b * LEAF + h * HALF
            values = x_ref[:, at : at + HALF].astype(jnp.float32)
            scaled = values * (weight_ref[0:1, at : at + HALF] * FOLD)
            first = (b % PART) * 32 + h * SIDES
            table_ref[b // PART, first : first + SIDES, :] = scaled.astype(jnp.bfloat16)
    for q in range(boxes // PART):
        table_ref[q, 32 * PART :, :] = jnp.exp2(CODE * (source_ref[q] - 0.5)).astype(jnp.bfloat16)

    sub = lax.broadcasted_iota(jnp.int32, (8, LEAF), 0)

    def one(b, carry):
        point = (target_ref[b] - 0.5) * CYCLES
        high, low = split(point)
        whole = high + low
        square = whole * whole
        norm = square[0:1] + square[1:2] + square[2:3]
        n1, rest = split(norm)
        n2, n3 = split(norm - n1)
        del rest
        last = jnp.where(sub == 0, n1, jnp.where(sub == 1, n2, jnp.where(sub == 2, n3, 0.0)))
        for h in range(2):
            here = (sub >= 4 * h) & (sub < 4 * h + 3)
            one_row = jnp.where(sub == 4 * h + 3, 1.0, 0.0)
            blocks = [
                jnp.where(here, -2.0 * high, one_row),
                jnp.where(here, -2.0 * low, one_row),
                jnp.where(here, -2.0 * high, one_row),
                jnp.where(here, -2.0 * low, 0.0),
                last,
                jnp.zeros_like(last),
            ]
            feature_ref[b, :, h * LEAF : (h + 1) * LEAF] = jnp.concatenate(blocks, 0).astype(
                jnp.bfloat16
            )
        return carry

    lax.fori_loop(0, boxes, one, 0)


def pack_kernel(asked_ref, table_ref, *out_refs):
    step = pl.program_id(0)
    block = out_refs[0].shape[0]

    def one(d, carry):
        for part, out_ref in enumerate(out_refs):
            coded = []
            for p in range(PART):
                q = asked_ref[step * block + d, part * PART + p]
                pair, side = q // PART, q % PART
                out_ref[d, 32 * p : 32 * (p + 1), :] = table_ref[
                    pair, pl.ds(pl.multiple_of(side * 32, 32), 32), :
                ]
                both = table_ref[pair, 32 * PART :, :].astype(jnp.float32)
                coded.append(jnp.where(side == 0, both[0:8], both[8:16]))
            out_ref[d, 32 * PART :, :] = jnp.concatenate(coded, 0).astype(jnp.bfloat16)
        return carry

    lax.fori_loop(0, block, one, 0)


def work_group(entry, source_ref, feature_ref, total_ref, square_ref, kernel_ref):
    sub = lax.broadcasted_iota(jnp.int32, (8, HALF), 0)
    norm_row = (sub % 4) == 3
    places = [entry(g) for g in range(GROUP)]
    for g, (target, place, side) in enumerate(places):
        both = source_ref[place, 32 * PART :, :].astype(jnp.float32)
        coded = jnp.where(side == 0, both[0:8], both[8:16])
        point = jnp.log2(coded) * (CYCLES / CODE)
        high, low = split(point)
        whole = high + low
        square = whole * whole
        norm = (
            pltpu.roll(square, 1, 0) + pltpu.roll(square, 2, 0) + pltpu.roll(square, 3, 0)
        )
        n1 = norm.astype(jnp.bfloat16).astype(jnp.float32)
        n2, n3 = split(norm - n1)
        ones = jnp.ones_like(norm)
        blocks = [
            jnp.where(norm_row, n1, high),
            jnp.where(norm_row, n2, high),
            jnp.where(norm_row, n3, low),
            low,
            ones,
            ones,
        ]
        features = jnp.concatenate(blocks, 0).T.astype(jnp.bfloat16)
        square_ref[g] = jnp.dot(
            features, feature_ref[target], preferred_element_type=jnp.float32
        )
    for g, (target, place, side) in enumerate(places):
        for h in range(2):
            for r in range(0, HALF, 32):
                d = jnp.maximum(square_ref[g, r : r + 32, h * LEAF : (h + 1) * LEAF], 1e-12)
                turns = d * lax.rsqrt(d)
                turns = turns - ((turns + MAGIC) - MAGIC)
                z = turns * turns
                value = z + MONIC[-1]
                for c in MONIC[-2::-1]:
                    value = value * z + c
                value = value * lax.rsqrt(d + SOFTEN)
                kernel_ref[g, h * HALF + r : h * HALF + r + 32, :] = value.astype(jnp.bfloat16)
        rows = source_ref[place, pl.ds(pl.multiple_of(side * 32, 32), 32), :]
        values = jnp.concatenate([rows[:SIDES], rows[SIDES:]], axis=1)
        total_ref[target] += jnp.dot(values, kernel_ref[g], preferred_element_type=jnp.float32)


def own_kernel(place_ref, table_ref, feature_ref, total_ref, list_ref, square_ref, kernel_ref):
    boxes, listed = place_ref.shape
    total_ref[...] = jnp.zeros_like(total_ref)

    def group(k, carry):
        def entry(g):
            b = k * GROUP + g
            return b, b // PART, b % PART

        work_group(entry, table_ref, feature_ref, total_ref, square_ref, kernel_ref)
        return carry

    lax.fori_loop(0, boxes // GROUP, group, 0)

    parts = list_ref.shape[0]

    def scan(b, counts):
        counts = list(counts)
        for i in range(listed):
            place = place_ref[b, i]
            part = (place % SLOTS) // PART
            code = b * 1024 + place
            for c in range(parts):
                list_ref[c, counts[c]] = code
                counts[c] = counts[c] + jnp.where(part == c, 1, 0)
        return tuple(counts)

    counts = lax.fori_loop(0, boxes, scan, (jnp.int32(0),) * parts)
    for c in range(parts):
        for k in range(GROUP):
            list_ref[c, counts[c] + k] = boxes * 1024
        list_ref[c, list_ref.shape[1] - 1] = (counts[c] + GROUP - 1) // GROUP


def near_kernel(part, list_ref, got_ref, feature_ref, old_ref, total_ref, square_ref, kernel_ref):
    total_ref[...] = old_ref[...]

    def group(k, carry):
        def entry(g):
            code = list_ref[part, k * GROUP + g]
            target, place = code // 1024, code % 1024
            return target, place // SLOTS, place % PART

        work_group(entry, got_ref, feature_ref, total_ref, square_ref, kernel_ref)
        return carry

    lax.fori_loop(0, list_ref[part, list_ref.shape[1] - 1], group, 0)


def far_kernel(
    dev0_ref, box0_ref, dev1_ref, box1_ref,
    table_ref, couple0_ref, couple1_ref, transfer_ref, basis_ref, near_ref, out_ref,
    stack_ref, up_ref,
):
    p = pl.program_id(0)
    listed = dev0_ref.shape[1]
    lane = lax.broadcasted_iota(jnp.int32, (SIDES, HALF), 1)
    share = table_ref.shape[0] // 128

    def piece(place, index, want):
        tile = table_ref[place].astype(jnp.float32)
        turn = jnp.where(index % 2 == want, 0, WIDTH)
        return pltpu.roll(tile, turn, 1)

    def gather(dev_ref, box_ref, row, first, into_ref, at):
        for j in range(0, listed, 2):
            parts = []
            for k in range(2):
                if j + k < listed:
                    index = box_ref[row, j + k]
                    parts.append(piece(dev_ref[row, j + k] * share + first + index // 2, index, k))
                else:
                    parts.append(jnp.zeros((SIDES, HALF), jnp.float32))
            into_ref[pl.ds(at, SIDES), j * WIDTH : (j + 2) * WIDTH] = jnp.where(
                lane < WIDTH, parts[0], parts[1]
            ).astype(jnp.bfloat16)

    def leaf(i, carry):
        gather(dev0_ref, box0_ref, 8 * p + i, 0, stack_ref, pl.multiple_of(i * SIDES, SIDES))
        return carry

    lax.fori_loop(0, 8, leaf, 0)
    gather(dev1_ref, box1_ref, p, 16, up_ref, 0)
    length = listed * WIDTH
    parent_far = contract_last(up_ref[:, :length], couple1_ref[0]).astype(jnp.bfloat16)
    down = jnp.dot(parent_far, transfer_ref[0], preferred_element_type=jnp.float32)
    for half in range(2):
        matrices = couple0_ref[4 * half : 4 * half + 4].reshape(4 * WIDTH, length)
        stacked = stack_ref[4 * half * SIDES : 4 * (half + 1) * SIDES, :length]
        product = contract_last(stacked, matrices)
        for k in range(4):
            i = 4 * half + k
            field = (
                product[k * SIDES : (k + 1) * SIDES, k * WIDTH : (k + 1) * WIDTH]
                + down[:, i * WIDTH : (i + 1) * WIDTH]
            ).astype(jnp.bfloat16)
            far = jnp.dot(field, basis_ref[i], preferred_element_type=jnp.float32)
            out_ref[:, i * LEAF : (i + 1) * LEAF] = (far + near_ref[i]).astype(jnp.bfloat16)


def on_device(
    x_values, coords, weights, basis, transfer, couple0, couple1,
    first_far_partner_device, far0_box, far1_dev, far1_box, near_partner_device, near_box,
):
    devices = lax.axis_size(AXES)
    boxes = basis.shape[0]
    parents = transfer.shape[0]
    listed = near_partner_device.shape[1]
    params = functools.partial(pltpu.CompilerParams, vmem_limit_bytes=48 * 2**20)
    rows = boxes // 2 + parents // 2

    coef = pl.pallas_call(
        coef_kernel,
        out_shape=jax.ShapeDtypeStruct((rows, SIDES, HALF), jnp.bfloat16),
        in_specs=[vmem()] * 3,
        out_specs=vmem(),
        compiler_params=params(),
        name="coef",
    )(x_values, basis, transfer)
    table = lax.all_gather(coef, AXES, axis=0, tiled=True)

    asked, place = pl.pallas_call(
        plan_kernel,
        out_shape=(
            jax.ShapeDtypeStruct((devices, devices), jnp.int32),
            jax.ShapeDtypeStruct((boxes, listed), jnp.int32),
        ),
        in_specs=[vmem()] * 2,
        out_specs=(vmem(), vmem()),
        compiler_params=params(),
        name="plan",
    )(near_partner_device, near_box)
    requests = lax.all_to_all(
        asked.reshape(devices, 1, devices), AXES, split_axis=0, concat_axis=0, tiled=True
    ).reshape(devices, devices)

    halves = coords.reshape(3, boxes, 2, HALF).transpose(1, 2, 0, 3)
    source = jnp.pad(halves, ((0, 0), (0, 0), (0, 1), (0, 0)), constant_values=0.5)
    source = source.reshape(boxes // PART, 8 * PART, HALF)
    target = jnp.pad(coords.reshape(3, boxes, LEAF), ((0, 1), (0, 0), (0, 0)), constant_values=0.5)
    target = target.transpose(1, 0, 2)
    target = jnp.concatenate([target, target], axis=1)
    own, features = pl.pallas_call(
        prepare_kernel,
        out_shape=(
            jax.ShapeDtypeStruct((boxes // PART, ROWS, HALF), jnp.bfloat16),
            jax.ShapeDtypeStruct((boxes + 1, FEATURES, 2 * LEAF), jnp.bfloat16),
        ),
        in_specs=[vmem()] * 4,
        out_specs=(vmem(), vmem()),
        compiler_params=params(),
        name="prepare",
    )(x_values, weights.reshape(1, boxes * LEAF), source, target)

    scratch = [
        pltpu.VMEM((GROUP, HALF, 2 * LEAF), jnp.float32),
        pltpu.VMEM((GROUP, LEAF, LEAF), jnp.bfloat16),
    ]
    parts = SLOTS // PART
    pairs = boxes * LEAF * LEAF
    total_shape = jax.ShapeDtypeStruct((boxes + 1, SIDES, LEAF), jnp.float32)
    near, listing = pl.pallas_call(
        own_kernel,
        out_shape=(total_shape, jax.ShapeDtypeStruct((parts, 384), jnp.int32)),
        in_specs=[smem(), vmem(), vmem()],
        out_specs=(vmem(), smem()),
        scratch_shapes=scratch,
        compiler_params=params(),
        cost_estimate=pl.CostEstimate(
            flops=40 * pairs, bytes_accessed=4 << 20, transcendentals=2 * pairs
        ),
        name="own",
    )(place, own, features)

    per_step = 16
    packed = pl.pallas_call(
        pack_kernel,
        out_shape=[jax.ShapeDtypeStruct((devices, ROWS, HALF), jnp.bfloat16)] * parts,
        grid=(devices // per_step,),
        in_specs=[smem(), pl.BlockSpec((boxes // PART, ROWS, HALF), lambda i: (0, 0, 0))],
        out_specs=[pl.BlockSpec((per_step, ROWS, HALF), lambda i: (i, 0, 0))] * parts,
        compiler_params=params(),
        name="pack",
    )(requests, own)

    for part in range(parts):
        got = lax.all_to_all(packed[part], AXES, split_axis=0, concat_axis=0, tiled=True)
        near = pl.pallas_call(
            functools.partial(near_kernel, part),
            out_shape=total_shape,
            in_specs=[smem(), vmem(), vmem(), vmem()],
            out_specs=vmem(),
            scratch_shapes=scratch,
            input_output_aliases={3: 0},
            compiler_params=params(),
            cost_estimate=pl.CostEstimate(
                flops=160 * pairs, bytes_accessed=8 << 20, transcendentals=8 * pairs
            ),
            name="near",
        )(listing, got, features, near)

    length = couple0.shape[2]
    padded = (length + HALF - 1) // HALF * HALF
    return pl.pallas_call(
        far_kernel,
        out_shape=jax.ShapeDtypeStruct((SIDES, boxes * LEAF), jnp.bfloat16),
        grid=(parents,),
        in_specs=[
            smem(), smem(), smem(), smem(),
            pl.BlockSpec((devices * rows, SIDES, HALF), lambda i: (0, 0, 0)),
            pl.BlockSpec((8, WIDTH, length), lambda i: (i, 0, 0)),
            pl.BlockSpec((1, WIDTH, length), lambda i: (i, 0, 0)),
            pl.BlockSpec((1, WIDTH, 8 * WIDTH), lambda i: (i, 0, 0)),
            pl.BlockSpec((8, WIDTH, LEAF), lambda i: (i, 0, 0)),
            pl.BlockSpec((8, SIDES, LEAF), lambda i: (i, 0, 0)),
        ],
        out_specs=pl.BlockSpec((SIDES, 8 * LEAF), lambda i: (0, i)),
        scratch_shapes=[
            pltpu.VMEM((8 * SIDES, padded), jnp.bfloat16),
            pltpu.VMEM((SIDES, padded), jnp.bfloat16),
        ],
        compiler_params=params(),
        name="far",
    )(
        first_far_partner_device, far0_box, far1_dev, far1_box,
        table, couple0, couple1, transfer, basis, near,
    )


def solution(mesh):
    placed = (
        P(None, AXES),
        P(None, AXES),
        P(AXES),
        P(AXES, None, None),
        P(AXES, None, None),
        P(AXES, None, None),
        P(AXES, None, None),
        P(AXES, None),
        P(AXES, None),
        P(AXES, None),
        P(AXES, None),
        P(AXES, None),
        P(AXES, None),
    )
    return jax.shard_map(
        on_device, mesh=mesh, in_specs=placed, out_specs=P(None, AXES), check_vma=False
    )
```

time: 636 us -> 187 us (0.29); the launches traced: 625 us -> 186 us
  matrix products: 311 us -> 0 us
  local copies, waits for them, and re-layouts: 168 us -> 10.7 us
  Pallas kernels: 0 us -> 98.1 us
  waiting for transfers between devices: 91.7 us -> 5.5 us
  blocking collectives: 0 us -> 41.4 us
  starting transfers between devices: 47.7 us -> 17.1 us
  between operations: 0.71 us -> 13.6 us
    dot_general x12 -> x0, matrix products: 311 us -> none  [the longest x8 303 us: kernel_block(): jnp.einsum('qwoj,qwkj->qko', kernel_evaluator.astype(jnp.bfloat16), value...]
    pallas_call x0 -> x8, Pallas kernels: none -> 98.1 us  [the longest x2 56.1 us: on_device(): pl.pallas_call(functools.partial(near_kernel, part), out_shape=total_shap...]
    all_to_all x7 -> x2, waiting for transfers between devices: 91.7 us -> 5.48 us  [the longest x1 5.48 us: on_device(): lax.all_to_all(asked.reshape(devices, 1, devices), AXES, split_axis=0, co...]
    scatter x3 -> x0, local copies, waits for them, and re-layouts: 61.3 us -> none  [request_buffer(): return empty.at[flat_owner, position].set(payload)]
    gather x11 -> x0, local copies, waits for them, and re-layouts: 49.5 us -> none  [the longest x1 19.2 us: fetch_leaf(): replies[flat_owner, position].reshape(count, listed, coefficients.shape[1])]
    all_to_all x0 -> x1, blocking collectives: none -> 41.4 us  [on_device(): lax.all_to_all(packed[part], AXES, split_axis=0, concat_axis=0, tiled=True)]
    all_to_all x7 -> x2, starting transfers between devices: 47.7 us -> 17.1 us  [the longest x1 11.5 us: on_device(): lax.all_to_all(asked.reshape(devices, 1, devices), AXES, split_axis=0, co...]
    reshape x14 -> x0, local copies, waits for them, and re-layouts: 19.3 us -> none  [the longest x2 15.4 us: couple_level(): stacked = wanted.reshape(count, listed, sides, width).transpose(0, 2, 1,...]
  transfers between devices with their start and end apart: 7 -> 3, of which waited for: 5 -> 1; matrix products, arithmetic and copies ran while one was open for 23% -> 2% of each run, Pallas kernels for 0% -> 42%
where the time goes in v1:
time: 187 us; the launch traced here: 186 us
  Pallas kernels  98.1 us (52%)
  blocking collectives  41.4 us (22%)
  starting transfers between devices  17.1 us (9%)
  between operations  13.6 us (7%)
  local copies, waits for them, and re-layouts  10.7 us (6%)
  waiting for transfers between devices  5.5 us (3%)
    pallas_call x2, Pallas kernels, on_device(): pl.pallas_call(functools.partial(near_kernel, part), out_shape=total_shap...  56.1 us
    all_to_all x1, blocking collectives, on_device(): lax.all_to_all(packed[part], AXES, split_axis=0, concat_axis=0, tiled=True)  41.4 us
    pallas_call x1, Pallas kernels, on_device(): pl.pallas_call(far_kernel, out_shape=jax.ShapeDtypeStruct((SIDES, boxes *...  19.4 us
    all_to_all x1, starting transfers between devices, on_device(): lax.all_to_all(asked.reshape(devices, 1, devices), AXES, split_axis=0, co...  11.5 us
    pallas_call x1, Pallas kernels, on_device(): pl.pallas_call(own_kernel, out_shape=(total_shape, jax.ShapeDtypeStruct((...  11.3 us
    unnamed x32, local copies, waits for them, and re-layouts  8.87 us
    pallas_call x1, Pallas kernels, on_device(): pl.pallas_call(pack_kernel, out_shape=[jax.ShapeDtypeStruct((devices, ROW...  8.11 us
    all_to_all x1, starting transfers between devices, on_device(): lax.all_to_all(packed[part], AXES, split_axis=0, concat_axis=0, tiled=True)  5.57 us
  transfers between devices with their start and end apart: 3, of which 1 were waited for; matrix products, arithmetic and copies ran while one was open for 2% of the time, Pallas kernels for 42%

profile of v1, /device:TPU:1, one launch (start us, length us, event | category | flops | bytes accessed | tf_op | source)
XLA Modules:
  0.0 186.5 jit_solution(5444661685058864478)
XLA Ops:
  6.5 0.0 all-gather.2.cloned.1.call-start
  6.5 0.0 copy-start
  6.5 1.2 copy-done
  7.8 0.9 copy-done.2
  8.7 0.0 copy-start.4
  8.7 0.9 copy-done.4
  9.7 0.0 copy-start.5
  9.7 0.0 copy-start.7
  9.7 1.3 coef.1
  11.0 0.0 all-gather.2.cloned.1.call-update
  11.0 0.8 copy.19.dev_ref
  11.7 0.8 copy.20.box_ref
  12.5 1.0 plan.1
  13.5 11.5 %all-to-all-start = ((s32[128,1,128]{2,1,0:T(1,128)}), s32[128,1,128]{2,1,0:T(1,128)S(1)}, u32[]{:S(2)}, u32[]{:S(2)}) async-start(s32[128,1,128]{2,1,0:T(1,128)} %bitcast.7), calls=%async_computation | async-start | bytes 131072 | tf_op jit(solution)/shard_map/all_to_all | solution.py:358
  25.0 0.9 pad.8
  25.9 0.9 pad_bitcast_fusion
  26.9 0.0 copy-done.5
  26.9 0.0 copy-done.7
  26.9 0.9 prepare.1
  27.9 0.0 copy-start.12
  27.9 1.2 copy-done.12
  29.1 5.5 %all-to-all-done = s32[128,1,128]{2,1,0:T(1,128)S(1)} async-done(((s32[128,1,128]{2,1,0:T(1,128)}), s32[128,1,128]{2,1,0:T(1,128)S(1)}, u32[]{:S(2)}, u32[]{:S(2)}) %all-to-all-start) | async-done | bytes 65568 | tf_op jit(solution)/shard_map/all_to_all | solution.py:358
  34.6 8.1 %pack.1 = (bf16[128,80,128]{2,1,0:T(8,128)(2,1)S(1)}, bf16[128,80,128]{2,1,0:T(8,128)(2,1)}) custom-call(s32[128,128]{1,0:T(8,128)S(1)} %bitcast.13, bf16[16,80,128]{2,1,0:T(8,128)(2,1)S(1)} %get-tuple-element.14.table_ref), custom_call_target="tpu_custom_call" | custom-call | tf_op jit(solution)/shard_map/pack/pallas_call | solution.py:401
  42.7 41.4 %all_to_all.15.got_ref = bf16[128,80,128]{2,1,0:T(8,128)(2,1)S(1)} all-to-all(bf16[128,80,128]{2,1,0:T(8,128)(2,1)S(1)} %get-tuple-element.19), channel_id=1, replica_groups=mesh['row'=8,'col'=16] {'row','col'}, dimensions={0} | all-to-all | bytes 5242880 | tf_op jit(solution)/shard_map/all_to_all | solution.py:412
  84.1 5.6 %all-to-all-start.1 = ((bf16[128,80,128]{2,1,0:T(8,128)(2,1)}), bf16[128,80,128]{2,1,0:T(8,128)(2,1)}, u32[]{:S(2)}, u32[]{:S(2)}) async-start(bf16[128,80,128]{2,1,0:T(8,128)(2,1)} %get-tuple-element.18), calls=%async_computation.1 | async-start | bytes 5242880 | tf_op jit(solution)/shard_map/all_to_all | solution.py:412
  89.7 0.0 copy-start.13
  89.7 1.4 copy-done.13
  91.1 11.3 %own.1 = (f32[33,16,256]{2,1,0:T(8,128)S(1)}, s32[2,384]{1,0:T(2,128)S(1)}) custom-call(s32[32,8]{1,0:T(8,128)S(1)} %get-tuple-element.13.place_ref, bf16[16,80,128]{2,1,0:T(8,128)(2,1)S(1)} %get-tuple-element.14.table_ref, bf16[33,48,512]{2,1,0:T(8,128)(2,1)S(1)} %copy-done.13), custom_call_target="tpu_custom_call" | custom-call | flops 83886080 | bytes 4194304 | tf_op jit(solution)/shard_map/own/pallas_call | solution.py:387
  102.4 49.4 %near.2.old_ref = f32[33,16,256]{2,1,0:T(8,128)S(1)} custom-call(s32[2,384]{1,0:T(2,128)S(1)} %get-tuple-element.16.list_ref, bf16[128,80,128]{2,1,0:T(8,128)(2,1)S(1)} %all_to_all.15.got_ref, bf16[33,48,512]{2,1,0:T(8,128)(2,1)S(1)} %copy-done.13, f32[33,16,256]{2,1,0:T(8,128)S(1)} %get-tuple-element.20.old_ref), custom_call_target="tpu_custom_call", output_to_operand_aliasing={{}: (3, {})} | custom-call | flops 335544320 | bytes 8388608 | tf_op jit(solution)/shard_map/near/pallas_call | solution.py:413
  151.8 0.0 copy-start.1
  151.8 0.0 copy-start.3
  151.8 0.0 copy-start.6
  151.8 0.0 copy-start.8
  151.8 0.0 copy-start.9
  151.8 0.0 copy-start.10
  151.8 0.0 copy-start.11
  151.8 0.0 all-to-all-done.1.got_ref
  151.8 0.0 copy-start.14
  151.9 1.6 copy-done.14
  153.4 6.7 %near.3.near_ref = f32[33,16,256]{2,1,0:T(8,128)S(1)} custom-call(s32[2,384]{1,0:T(2,128)S(1)} %get-tuple-element.16.list_ref, bf16[128,80,128]{2,1,0:T(8,128)(2,1)} %all-to-all-done.1.got_ref, bf16[33,48,512]{2,1,0:T(8,128)(2,1)S(1)} %copy-done.14, f32[33,16,256]{2,1,0:T(8,128)S(1)} %near.2.old_ref), custom_call_target="tpu_custom_call", output_to_operand_aliasing={{}: (3, {})} | custom-call | flops 335544320 | bytes 8388608 | tf_op jit(solution)/shard_map/near/pallas_call | solution.py:413
  160.1 0.0 copy-done.1
  160.1 0.0 copy-done.3
  160.1 0.0 copy-done.6
  160.1 0.0 copy-done.8
  160.1 0.0 copy-done.9
  160.1 0.0 copy-done.10
  160.2 0.0 copy-done.11
  160.2 19.4 %far.1 = bf16[16,8192]{1,0:T(8,128)(2,1)} custom-call(s32[32,27]{1,0:T(8,128)S(1)} %copy-done.8, s32[32,27]{1,0:T(8,128)S(1)} %copy-done.9, s32[4,27]{1,0:T(4,128)S(1)} %copy-done.10, s32[4,27]{1,0:T(4,128)S(1)} %copy-done.11, bf16[2304,16,128]{2,1,0:T(8,128)(2,1)} %all-gather.2.cloned.1.call-done.table_ref, bf16[32,64,1728]{2,1,0:T(8,128)(2,1)} %couple0_ref.1, ...), custom_call_target="tpu_custom_call" | custom-call | tf_op jit(solution)/shard_map/far/pallas_call | solution.py:429
  (3 shorter events, 0.1 us)
Async XLA Ops:
  6.5 153.6 %all-gather.2.cloned.1.call-start = ((), (), s32[]{:S(2)}) async-start(), calls=%async_computation.3 | async-start | bytes 9510912 | tf_op jit(solution)/shard_map/all_gather | solution.py:345
  6.5 1.2 copy-start
  7.8 0.9 copy-start.2
  8.7 0.9 copy-start.4
  9.7 17.3 %copy-start.5 = (bf16[16,8192]{1,0:T(8,128)(2,1)S(1)}, bf16[16,8192]{1,0:T(8,128)(2,1)}, u32[]{:S(2)}) copy-start(bf16[16,8192]{1,0:T(8,128)(2,1)} %x_ref.3) | copy-start | bytes 786436
  9.7 17.3 %copy-start.7 = (f32[8192]{0:T(1024)S(1)}, f32[8192]{0:T(1024)}, u32[]{:S(2)}) copy-start(f32[8192]{0:T(1024)} %param.15) | copy-start | bytes 98308
  13.5 21.1 %all-to-all-start = ((s32[128,1,128]{2,1,0:T(1,128)}), s32[128,1,128]{2,1,0:T(1,128)S(1)}, u32[]{:S(2)}, u32[]{:S(2)}) async-start(s32[128,1,128]{2,1,0:T(1,128)} %bitcast.7), calls=%async_computation | async-start | bytes 131072 | tf_op jit(solution)/shard_map/all_to_all | solution.py:358
  27.9 1.2 copy-start.12
  84.1 67.8 %all-to-all-start.1 = ((bf16[128,80,128]{2,1,0:T(8,128)(2,1)}), bf16[128,80,128]{2,1,0:T(8,128)(2,1)}, u32[]{:S(2)}, u32[]{:S(2)}) async-start(bf16[128,80,128]{2,1,0:T(8,128)(2,1)} %get-tuple-element.18), calls=%async_computation.1 | async-start | bytes 5242880 | tf_op jit(solution)/shard_map/all_to_all | solution.py:412
  89.7 1.4 copy-start.13
  151.8 8.3 %copy-start.1 = (bf16[32,64,256]{2,1,0:T(8,128)(2,1)S(1)}, bf16[32,64,256]{2,1,0:T(8,128)(2,1)}, u32[]{:S(2)}) copy-start(bf16[32,64,256]{2,1,0:T(8,128)(2,1)} %basis_ref.3) | copy-start | bytes 3145732
  151.8 8.3 %copy-start.3 = (bf16[4,64,512]{2,1,0:T(8,128)(2,1)S(1)}, bf16[4,64,512]{2,1,0:T(8,128)(2,1)}, u32[]{:S(2)}) copy-start(bf16[4,64,512]{2,1,0:T(8,128)(2,1)} %transfer_ref.3) | copy-start | bytes 786436
  151.8 8.3 %copy-start.6 = (bf16[4,64,1728]{2,1,0:T(8,128)(2,1)S(1)}, bf16[4,64,1728]{2,1,0:T(8,128)(2,1)}, u32[]{:S(2)}) copy-start(bf16[4,64,1728]{2,1,0:T(8,128)(2,1)} %couple1_ref.1) | copy-start | bytes 2654212
  151.8 8.3 %copy-start.8 = (s32[32,27]{1,0:T(8,128)S(1)}, s32[32,27]{1,0:T(8,128)}, u32[]{:S(2)}) copy-start(s32[32,27]{1,0:T(8,128)} %dev0_ref.1) | copy-start | bytes 10372
  151.8 8.3 %copy-start.9 = (s32[32,27]{1,0:T(8,128)S(1)}, s32[32,27]{1,0:T(8,128)}, u32[]{:S(2)}) copy-start(s32[32,27]{1,0:T(8,128)} %box0_ref.1) | copy-start | bytes 10372
  151.8 8.3 %copy-start.10 = (s32[4,27]{1,0:T(4,128)S(1)}, s32[4,27]{1,0:T(4,128)}, u32[]{:S(2)}) copy-start(s32[4,27]{1,0:T(4,128)} %dev1_ref.1) | copy-start | bytes 1300
  151.8 8.3 %copy-start.11 = (s32[4,27]{1,0:T(4,128)S(1)}, s32[4,27]{1,0:T(4,128)}, u32[]{:S(2)}) copy-start(s32[4,27]{1,0:T(4,128)} %box1_ref.1) | copy-start | bytes 1300
  151.8 1.6 copy-start.14
Sparse Core Ops, SparseCore 0:
  11.1 120.4 all-gather.1

commit v2 on v1

v2 whole, which is shorter than its diff:
```python
import functools
import math

import jax
import jax.numpy as jnp
import numpy as np
from jax import lax
from jax.experimental import pallas as pl
from jax.experimental.pallas import tpu as pltpu
from jax.sharding import PartitionSpec as P

AXES = ("row", "col")
LEAF = 256
HALF = 128
WIDTH = 64
SIDES = 16
SLOTS = 4
PART = 2
ROWS = 40 * PART
FEATURES = 48
GROUP = 8
BIAS = 1e-5
CODE = 248.0
CYCLES = 20.0 / (2.0 * math.pi)
SOFTEN = 0.01 * CYCLES * CYCLES


def cosine_polynomial(degree):
    fit = np.polynomial.chebyshev.Chebyshev.interpolate(
        lambda z: np.cos(2 * np.pi * np.sqrt(np.maximum(z, 0.0))), degree, [0.0, 0.25]
    )
    return [float(c) for c in fit.convert(kind=np.polynomial.Polynomial).coef]


COSINE = cosine_polynomial(4)
LEAD = COSINE[-1]
MONIC = [c / LEAD for c in COSINE[:-1]]
FOLD = LEAD * CYCLES


def split(value):
    high = value.astype(jnp.bfloat16).astype(jnp.float32)
    low = (value - high).astype(jnp.bfloat16).astype(jnp.float32)
    return high, low


def contract_last(a, b):
    return lax.dot_general(a, b, (((1,), (1,)), ((), ())), preferred_element_type=jnp.float32)


def vmem():
    return pl.BlockSpec(memory_space=pltpu.VMEM)


def smem():
    return pl.BlockSpec(memory_space=pltpu.SMEM)


def coef_kernel(x_ref, basis_ref, transfer_ref, out_ref):
    boxes = basis_ref.shape[0]
    parents = transfer_ref.shape[0]
    leaf = []
    for b in range(boxes):
        c = contract_last(x_ref[:, b * LEAF : (b + 1) * LEAF], basis_ref[b])
        leaf.append(c)
        if b % 2:
            out_ref[b // 2] = jnp.concatenate([leaf[b - 1], c], axis=1).astype(jnp.bfloat16)
    up = []
    for p in range(parents):
        children = jnp.concatenate([out_ref[4 * p + i] for i in range(4)], axis=1)
        up.append(contract_last(children, transfer_ref[p]))
        if p % 2:
            out_ref[boxes // 2 + p // 2] = jnp.concatenate([up[p - 1], up[p]], axis=1).astype(
                jnp.bfloat16
            )


def plan_kernel(dev_ref, box_ref, asked_ref, place_ref):
    listed, count = dev_ref.shape
    devices = asked_ref.shape[0]
    owner = lax.broadcasted_iota(jnp.int32, (devices, count), 0)
    dev, box = dev_ref[...], box_ref[...]
    named = jnp.zeros((devices, count), jnp.float32)
    wanted = jnp.zeros((devices, count), jnp.float32)
    hits = []
    for i in range(listed):
        hit = (dev[i : i + 1] == owner).astype(jnp.float32)
        hits.append(hit)
        named = named + hit
        wanted = wanted + hit * box[i : i + 1].astype(jnp.float32)
    row = lax.broadcasted_iota(jnp.int32, (count, count), 0)
    col = lax.broadcasted_iota(jnp.int32, (count, count), 1)
    before = jnp.dot(
        named.astype(jnp.bfloat16),
        (row < col).astype(jnp.bfloat16),
        preferred_element_type=jnp.float32,
    )
    slot = lax.broadcasted_iota(jnp.int32, (devices, devices), 1)
    asked = jnp.zeros((devices, devices), jnp.float32)
    for p in range(SLOTS):
        here = jnp.sum(
            jnp.where((before == p) & (named > 0), wanted, 0.0), axis=1, keepdims=True
        )
        asked = jnp.where(slot == p, here, asked)
    asked_ref[...] = asked.astype(jnp.int32)
    position = [jnp.sum(hit * before, axis=0, keepdims=True) for hit in hits]
    place_ref[...] = dev * SLOTS + jnp.concatenate(position, axis=0).astype(jnp.int32)


def prepare_kernel(
    x_ref, weight_ref, source_ref, target_ref, table_ref, coded_ref, feature_ref
):
    boxes = target_ref.shape[0]
    for b in range(boxes):
        for h in range(2):
            at = b * LEAF + h * HALF
            values = x_ref[:, at : at + HALF].astype(jnp.float32)
            scaled = values * (weight_ref[0:1, at : at + HALF] * FOLD)
            first = (b % PART) * 32 + h * SIDES
            table_ref[b // PART, first : first + SIDES, :] = scaled.astype(jnp.bfloat16)
    for q in range(boxes // PART):
        coded = jnp.exp2(CODE * (source_ref[q] - 0.5)).astype(jnp.bfloat16)
        table_ref[q, 32 * PART :, :] = coded
        for p in range(PART):
            coded_ref[PART * q + p] = coded.astype(jnp.float32)[8 * p : 8 * (p + 1)]

    sub = lax.broadcasted_iota(jnp.int32, (8, LEAF), 0)

    def one(b, carry):
        point = (target_ref[b] - 0.5) * CYCLES
        high, low = split(point)
        whole = high + low
        square = whole * whole
        norm = square[0:1] + square[1:2] + square[2:3] + BIAS
        n1 = norm.astype(jnp.bfloat16).astype(jnp.float32)
        n2, n3 = split(norm - n1)
        last = jnp.where(sub == 0, n1, jnp.where(sub == 1, n2, jnp.where(sub == 2, n3, 0.0)))
        for h in range(2):
            here = (sub >= 4 * h) & (sub < 4 * h + 3)
            one_row = jnp.where(sub == 4 * h + 3, 1.0, 0.0)
            blocks = [
                jnp.where(here, -2.0 * high, one_row),
                jnp.where(here, -2.0 * low, one_row),
                jnp.where(here, -2.0 * high, one_row),
                jnp.where(here, -2.0 * low, 0.0),
                last,
                jnp.zeros_like(last),
            ]
            feature_ref[b, :, h * LEAF : (h + 1) * LEAF] = jnp.concatenate(blocks, 0).astype(
                jnp.bfloat16
            )
        return carry

    lax.fori_loop(0, boxes, one, 0)


def pack_kernel(asked_ref, table_ref, coded_ref, *out_refs):
    step = pl.program_id(0)
    block = out_refs[0].shape[0]

    def one(k, carry):
        for d in (2 * k, 2 * k + 1):
            for part, out_ref in enumerate(out_refs):
                coded = []
                for p in range(PART):
                    q = asked_ref[step * block + d, part * PART + p]
                    side = pl.multiple_of(q % PART * 32, 32)
                    out_ref[d, 32 * p : 32 * (p + 1), :] = table_ref[q // PART, pl.ds(side, 32), :]
                    coded.append(coded_ref[q])
                out_ref[d, 32 * PART :, :] = jnp.concatenate(coded, 0).astype(jnp.bfloat16)
        return carry

    lax.fori_loop(0, block // 2, one, 0)


def start_pair(entry, source_ref, feature_ref, square_ref, g):
    target, place, side = entry
    sub = lax.broadcasted_iota(jnp.int32, (8, HALF), 0)
    norm_row = (sub % 4) == 3
    both = source_ref[place, 32 * PART :, :].astype(jnp.float32)
    coded = jnp.where(side == 0, both[0:8], both[8:16])
    point = jnp.log2(coded) * (CYCLES / CODE)
    high, low = split(point)
    whole = high + low
    square = whole * whole
    norm = pltpu.roll(square, 1, 0) + pltpu.roll(square, 2, 0) + pltpu.roll(square, 3, 0)
    n1 = norm.astype(jnp.bfloat16).astype(jnp.float32)
    n2, n3 = split(norm - n1)
    ones = jnp.ones_like(norm)
    blocks = [
        jnp.where(norm_row, n1, high),
        jnp.where(norm_row, n2, high),
        jnp.where(norm_row, n3, low),
        low,
        ones,
        ones,
    ]
    features = jnp.concatenate(blocks, 0).T.astype(jnp.bfloat16)
    square_ref[g] = jnp.dot(features, feature_ref[target], preferred_element_type=jnp.float32)


def values_of_pair(square_ref, kernel_ref, g):
    for h in range(2):
        for r in range(0, HALF, 32):
            d = square_ref[g, r : r + 32, h * LEAF : (h + 1) * LEAF]
            turns = d * lax.rsqrt(d)
            turns = turns - jnp.round(turns)
            z = turns * turns
            value = z + MONIC[-1]
            for c in MONIC[-2::-1]:
                value = value * z + c
            value = value * lax.rsqrt(d + SOFTEN)
            kernel_ref[g, h * HALF + r : h * HALF + r + 32, :] = value.astype(jnp.bfloat16)


def finish_pair(entry, source_ref, total_ref, kernel_ref, g):
    target, place, side = entry
    rows = source_ref[place, pl.ds(pl.multiple_of(side * 32, 32), 32), :]
    values = jnp.concatenate([rows[:SIDES], rows[SIDES:]], axis=1)
    total_ref[target] += jnp.dot(values, kernel_ref[g], preferred_element_type=jnp.float32)


def work(groups, entry, source_ref, feature_ref, total_ref, square_ref, kernel_ref):
    for g in range(GROUP):
        start_pair(entry(g), source_ref, feature_ref, square_ref, g)

    def body(k, carry):
        for half in range(2):
            at = (2 * k + half) * GROUP
            mine = half * GROUP
            for g in range(GROUP):
                start_pair(
                    entry(at + GROUP + g), source_ref, feature_ref, square_ref, GROUP - mine + g
                )
                values_of_pair(square_ref, kernel_ref, mine + g)
                if g:
                    finish_pair(entry(at + g - 1), source_ref, total_ref, kernel_ref, mine + g - 1)
            finish_pair(entry(at + GROUP - 1), source_ref, total_ref, kernel_ref, mine + GROUP - 1)
        return carry

    lax.fori_loop(0, groups, body, 0)


def own_kernel(place_ref, table_ref, feature_ref, total_ref, list_ref, square_ref, kernel_ref):
    listed, boxes = place_ref.shape
    total_ref[...] = jnp.zeros_like(total_ref)

    def entry(k):
        b = jnp.minimum(k, boxes - 1)
        return b, b // PART, b % PART

    groups = boxes // (2 * GROUP)
    work(groups, entry, table_ref, feature_ref, total_ref, square_ref, kernel_ref)

    parts = list_ref.shape[0]

    def scan(b, counts):
        counts = list(counts)
        for i in range(listed):
            place = place_ref[i, b]
            part = (place % SLOTS) // PART
            code = b * 1024 + place
            for c in range(parts):
                list_ref[c, counts[c]] = code
                counts[c] = counts[c] + jnp.where(part == c, 1, 0)
        return tuple(counts)

    counts = lax.fori_loop(0, boxes, scan, (jnp.int32(0),) * parts)
    for c in range(parts):
        for k in range(3 * GROUP):
            list_ref[c, counts[c] + k] = boxes * 1024
        list_ref[c, list_ref.shape[1] - 1] = (counts[c] + 2 * GROUP - 1) // (2 * GROUP)


def near_kernel(part, list_ref, got_ref, feature_ref, old_ref, total_ref, square_ref, kernel_ref):
    total_ref[...] = old_ref[...]

    def entry(k):
        code = list_ref[part, k]
        target, place = code // 1024, code % 1024
        return target, place // SLOTS, place % PART

    groups = list_ref[part, list_ref.shape[1] - 1]
    work(groups, entry, got_ref, feature_ref, total_ref, square_ref, kernel_ref)


def far_kernel(
    code0_ref, code1_ref, table_ref, couple0_ref, couple1_ref, transfer_ref, basis_ref, near_ref,
    out_ref, stack_ref, up_ref,
):
    listed = code0_ref.shape[1]
    length = listed * WIDTH
    lane = lax.broadcasted_iota(jnp.int32, (SIDES, HALF), 1)

    def piece(code_ref, row, j):
        code = code_ref[row, j]
        tile = table_ref[code // 2]
        return jnp.where((code + j) % 2 == 0, tile, pltpu.roll(tile, WIDTH, 1))

    def gather(code_ref, row, into_ref, at):
        for j in range(0, listed, 2):
            tile = piece(code_ref, row, j)
            if j + 1 < listed:
                tile = jnp.where(lane < WIDTH, tile, piece(code_ref, row, j + 1))
            into_ref[pl.ds(at, SIDES), j * WIDTH : (j + 2) * WIDTH] = tile

    def parent(p, carry):
        gather(code1_ref, p, up_ref, 0)
        for i in range(8):
            gather(code0_ref, 8 * p + i, stack_ref, i * SIDES)
        parent_far = contract_last(up_ref[:, :length], couple1_ref[p]).astype(jnp.bfloat16)
        down = jnp.dot(parent_far, transfer_ref[p], preferred_element_type=jnp.float32)
        for half in range(2):
            first = 8 * p + 4 * half
            matrices = couple0_ref[pl.ds(first, 4)].reshape(4 * WIDTH, length)
            stacked = stack_ref[4 * half * SIDES : 4 * (half + 1) * SIDES, :length]
            product = contract_last(stacked, matrices)
            for k in range(4):
                i = 4 * half + k
                field = (
                    product[k * SIDES : (k + 1) * SIDES, k * WIDTH : (k + 1) * WIDTH]
                    + down[:, i * WIDTH : (i + 1) * WIDTH]
                ).astype(jnp.bfloat16)
                far = jnp.dot(field, basis_ref[first + k], preferred_element_type=jnp.float32)
                at = pl.multiple_of((first + k) * LEAF, LEAF)
                out_ref[:, pl.ds(at, LEAF)] = (far + near_ref[first + k]).astype(jnp.bfloat16)
        return carry

    lax.fori_loop(0, transfer_ref.shape[0], parent, 0)


def on_device(
    x_values, coords, weights, basis, transfer, couple0, couple1,
    first_far_partner_device, far0_box, far1_dev, far1_box, near_partner_device, near_box,
):
    devices = lax.axis_size(AXES)
    boxes = basis.shape[0]
    parents = transfer.shape[0]
    listed = near_partner_device.shape[1]

    def params(mib):
        return pltpu.CompilerParams(vmem_limit_bytes=mib * 2**20)

    rows = boxes // 2 + parents // 2

    coef = pl.pallas_call(
        coef_kernel,
        out_shape=jax.ShapeDtypeStruct((rows, SIDES, HALF), jnp.bfloat16),
        in_specs=[vmem()] * 3,
        out_specs=vmem(),
        compiler_params=params(8),
        name="coef",
    )(x_values, basis, transfer)
    table = lax.all_gather(coef, AXES, axis=0, tiled=True)

    asked, place = pl.pallas_call(
        plan_kernel,
        out_shape=(
            jax.ShapeDtypeStruct((devices, devices), jnp.int32),
            jax.ShapeDtypeStruct((listed, boxes), jnp.int32),
        ),
        in_specs=[vmem()] * 2,
        out_specs=(vmem(), vmem()),
        compiler_params=params(8),
        name="plan",
    )(near_partner_device.T, near_box.T)
    requests = lax.all_to_all(
        asked.reshape(devices, 1, devices), AXES, split_axis=0, concat_axis=0, tiled=True
    ).reshape(devices, devices)

    halves = coords.reshape(3, boxes, 2, HALF).transpose(1, 2, 0, 3)
    source = jnp.pad(halves, ((0, 0), (0, 0), (0, 1), (0, 0)), constant_values=0.5)
    source = source.reshape(boxes // PART, 8 * PART, HALF)
    target = jnp.pad(coords.reshape(3, boxes, LEAF), ((0, 1), (0, 0), (0, 0)), constant_values=0.5)
    target = target.transpose(1, 0, 2)
    target = jnp.concatenate([target, target], axis=1)
    own, coded, features = pl.pallas_call(
        prepare_kernel,
        out_shape=(
            jax.ShapeDtypeStruct((boxes // PART, ROWS, HALF), jnp.bfloat16),
            jax.ShapeDtypeStruct((boxes, 8, HALF), jnp.float32),
            jax.ShapeDtypeStruct((boxes + 1, FEATURES, 2 * LEAF), jnp.bfloat16),
        ),
        in_specs=[vmem()] * 4,
        out_specs=(vmem(), vmem(), vmem()),
        compiler_params=params(8),
        name="prepare",
    )(x_values, weights.reshape(1, boxes * LEAF), source, target)

    scratch = [
        pltpu.VMEM((2 * GROUP, HALF, 2 * LEAF), jnp.float32),
        pltpu.VMEM((2 * GROUP, LEAF, LEAF), jnp.bfloat16),
    ]
    parts = SLOTS // PART
    pairs = boxes * LEAF * LEAF
    per_step = 16
    packed = pl.pallas_call(
        pack_kernel,
        out_shape=[jax.ShapeDtypeStruct((devices, ROWS, HALF), jnp.bfloat16)] * parts,
        grid=(devices // per_step,),
        in_specs=[
            smem(),
            pl.BlockSpec((boxes // PART, ROWS, HALF), lambda i: (0, 0, 0)),
            pl.BlockSpec((boxes, 8, HALF), lambda i: (0, 0, 0)),
        ],
        out_specs=[pl.BlockSpec((per_step, ROWS, HALF), lambda i: (i, 0, 0))] * parts,
        compiler_params=params(8),
        name="pack",
    )(requests, own, coded)

    packed, own, features = lax.optimization_barrier((packed, own, features))
    total_shape = jax.ShapeDtypeStruct((boxes + 1, SIDES, LEAF), jnp.float32)
    near, listing = pl.pallas_call(
        own_kernel,
        out_shape=(total_shape, jax.ShapeDtypeStruct((parts, 384), jnp.int32)),
        in_specs=[smem(), vmem(), vmem()],
        out_specs=(vmem(), smem()),
        scratch_shapes=scratch,
        compiler_params=params(12),
        cost_estimate=pl.CostEstimate(
            flops=40 * pairs, bytes_accessed=4 << 20, transcendentals=2 * pairs
        ),
        name="own",
    )(place, own, features)
    later, near, listing = lax.optimization_barrier((packed[1:], near, listing))
    packed = [packed[0], *later]

    for part in range(parts):
        got = lax.all_to_all(packed[part], AXES, split_axis=0, concat_axis=0, tiled=True)
        near = pl.pallas_call(
            functools.partial(near_kernel, part),
            out_shape=total_shape,
            in_specs=[smem(), vmem(), vmem(), vmem()],
            out_specs=vmem(),
            scratch_shapes=scratch,
            input_output_aliases={3: 0},
            compiler_params=params(12),
            cost_estimate=pl.CostEstimate(
                flops=160 * pairs, bytes_accessed=8 << 20, transcendentals=8 * pairs
            ),
            name="near",
        )(listing, got, features, near)

    padded = (couple0.shape[2] + HALF - 1) // HALF * HALF
    return pl.pallas_call(
        far_kernel,
        out_shape=jax.ShapeDtypeStruct((SIDES, boxes * LEAF), jnp.bfloat16),
        in_specs=[smem(), smem()] + [vmem()] * 6,
        out_specs=vmem(),
        scratch_shapes=[
            pltpu.VMEM((8 * SIDES, padded), jnp.bfloat16),
            pltpu.VMEM((SIDES, padded), jnp.bfloat16),
        ],
        compiler_params=params(8),
        name="far",
    )(
        first_far_partner_device * (2 * rows) + far0_box,
        far1_dev * (2 * rows) + boxes + far1_box,
        table, couple0, couple1, transfer, basis, near,
    )


def solution(mesh):
    placed = (
        P(None, AXES),
        P(None, AXES),
        P(AXES),
        P(AXES, None, None),
        P(AXES, None, None),
        P(AXES, None, None),
        P(AXES, None, None),
        P(AXES, None),
        P(AXES, None),
        P(AXES, None),
        P(AXES, None),
        P(AXES, None),
        P(AXES, None),
    )
    return jax.shard_map(
        on_device, mesh=mesh, in_specs=placed, out_specs=P(None, AXES), check_vma=False
    )
```

time: 187 us -> 173 us (0.925)
  blocking collectives: 41.4 us -> 0 us
  waiting for transfers between devices: 5.5 us -> 36.9 us
  Pallas kernels: 98.1 us -> 79.9 us
  local copies, waits for them, and re-layouts: 10.7 us -> 20.1 us
  starting transfers between devices: 17.1 us -> 21.5 us
    all_to_all x1 -> x0, blocking collectives: 41.4 us -> none  [on_device(): lax.all_to_all(packed[part], AXES, split_axis=0, concat_axis=0, tiled=True)]
    all_to_all x1 -> x2, waiting for transfers between devices: 0.01 us -> 31.4 us  [on_device(): lax.all_to_all(packed[part], AXES, split_axis=0, concat_axis=0, tiled=True)]
    pallas_call x2, Pallas kernels: 56.1 us -> 46.6 us  [on_device(): pl.pallas_call(functools.partial(near_kernel, part), out_shape=total_shap...]
    unnamed x32 -> x42, local copies, waits for them, and re-layouts: 8.87 us -> 18.2 us
    pallas_call x1, Pallas kernels: 19.4 us -> 12.4 us  [on_device(): pl.pallas_call(far_kernel, out_shape=jax.ShapeDtypeStruct((SIDES, boxes *...]
    all_to_all x1 -> x2, starting transfers between devices: 5.57 us -> 10 us  [on_device(): lax.all_to_all(packed[part], AXES, split_axis=0, concat_axis=0, tiled=True)]
  transfers between devices with their start and end apart: 3 -> 4, of which waited for: 1 -> 3; matrix products, arithmetic and copies ran while one was open for 2% -> 1% of each run, Pallas kernels for 42% -> 39%
where the time goes in v2:
time: 173 us; the launch traced here: 172 us
  Pallas kernels  79.9 us (46%)
  waiting for transfers between devices  36.9 us (21%)
  starting transfers between devices  21.5 us (12%)
  local copies, waits for them, and re-layouts  20.1 us (12%)
  between operations  13.6 us (8%)
    pallas_call x2, Pallas kernels, on_device(): pl.pallas_call(functools.partial(near_kernel, part), out_shape=total_shap...  46.6 us
    all_to_all x2, waiting for transfers between devices, on_device(): lax.all_to_all(packed[part], AXES, split_axis=0, concat_axis=0, tiled=True)  31.4 us
    unnamed x42, local copies, waits for them, and re-layouts  18.2 us
    pallas_call x1, Pallas kernels, on_device(): pl.pallas_call(far_kernel, out_shape=jax.ShapeDtypeStruct((SIDES, boxes *...  12.4 us
    all_to_all x1, starting transfers between devices, on_device(): lax.all_to_all(asked.reshape(devices, 1, devices), AXES, split_axis=0, co...  11.5 us
    pallas_call x1, Pallas kernels, on_device(): pl.pallas_call(own_kernel, out_shape=(total_shape, jax.ShapeDtypeStruct((...  10.3 us
    all_to_all x2, starting transfers between devices, on_device(): lax.all_to_all(packed[part], AXES, split_axis=0, concat_axis=0, tiled=True)  10 us
    pallas_call x1, Pallas kernels, on_device(): pl.pallas_call(pack_kernel, out_shape=[jax.ShapeDtypeStruct((devices, ROW...  7.44 us
  transfers between devices with their start and end apart: 4, of which 3 were waited for; matrix products, arithmetic and copies ran while one was open for 1% of the time, Pallas kernels for 39%

profile of v2, /device:TPU:1, one launch (start us, length us, event | category | flops | bytes accessed | tf_op | source)
XLA Modules:
  0.0 172.1 jit_solution(18348675416139092472)
XLA Ops:
  6.5 0.0 all-gather.2.cloned.1.call-start
  6.5 1.2 copy-done.2
  7.8 0.9 copy-done.5
  8.7 0.9 copy-done.7
  9.7 1.3 coef.1
  11.0 0.0 all-gather.2.cloned.1.call-update
  11.0 0.0 copy-start.11
  11.0 0.7 copy-done.11
  11.7 0.7 copy-done.12
  12.4 0.9 plan.1
  13.3 11.5 %all-to-all-start = ((s32[128,1,128]{2,1,0:T(1,128)}), s32[128,1,128]{2,1,0:T(1,128)S(1)}, u32[]{:S(2)}, u32[]{:S(2)}) async-start(s32[128,1,128]{2,1,0:T(1,128)} %bitcast.3), calls=%async_computation | async-start | bytes 131072 | tf_op jit(solution)/shard_map/all_to_all | solution.py:367
  24.8 0.9 pad.8
  25.7 0.9 pad_bitcast_fusion
  26.7 0.0 copy-done.8
  26.7 0.0 copy-done.10
  26.8 1.0 prepare.1
  27.7 1.2 copy-done.13
  28.9 5.5 %all-to-all-done = s32[128,1,128]{2,1,0:T(1,128)S(1)} async-done(((s32[128,1,128]{2,1,0:T(1,128)}), s32[128,1,128]{2,1,0:T(1,128)S(1)}, u32[]{:S(2)}, u32[]{:S(2)}) %all-to-all-start) | async-done | bytes 65568 | tf_op jit(solution)/shard_map/all_to_all | solution.py:367
  34.4 7.4 %pack.1 = (bf16[128,80,128]{2,1,0:T(8,128)(2,1)S(1)}, bf16[128,80,128]{2,1,0:T(8,128)(2,1)}) custom-call(s32[128,128]{1,0:T(8,128)S(1)} %bitcast.15, bf16[16,80,128]{2,1,0:T(8,128)(2,1)S(1)} %get-tuple-element.29.table_ref, f32[32,8,128]{2,1,0:T(8,128)S(1)} %get-tuple-element.23.coded_ref), custom_call_target="tpu_custom_call" | custom-call | tf_op jit(solution)/shard_map/pack/pallas_call | solution.py:397
  41.8 1.5 copy-done.4
  43.3 4.4 %all-to-all-start.2 = ((bf16[128,80,128]{2,1,0:T(8,128)(2,1)}), bf16[128,80,128]{2,1,0:T(8,128)(2,1)S(1)}, u32[]{:S(2)}, u32[]{:S(2)}) async-start(bf16[128,80,128]{2,1,0:T(8,128)(2,1)} %copy-done.4), calls=%async_computation.2 | async-start | bytes 5242880 | tf_op jit(solution)/shard_map/all_to_all | solution.py:429
  47.8 0.0 copy-start.14
  47.8 1.4 copy-done.14
  49.2 10.3 %own.1 = (f32[33,16,256]{2,1,0:T(8,128)S(1)}, s32[2,384]{1,0:T(2,128)S(1)}) custom-call(s32[8,32]{1,0:T(8,128)S(1)} %get-tuple-element.28.place_ref, bf16[16,80,128]{2,1,0:T(8,128)(2,1)S(1)} %get-tuple-element.29.table_ref, bf16[33,48,512]{2,1,0:T(8,128)(2,1)S(1)} %copy-done.14), custom_call_target="tpu_custom_call" | custom-call | flops 83886080 | bytes 4194304 | tf_op jit(solution)/shard_map/own/pallas_call | solution.py:413
  59.5 0.0 copy-start.19
  59.5 0.0 copy-start.20
  59.6 0.0 copy-start.17
  59.6 0.0 copy-start.18
  59.6 25.2 %all-to-all-done.2.got_ref = bf16[128,80,128]{2,1,0:T(8,128)(2,1)S(1)} async-done(((bf16[128,80,128]{2,1,0:T(8,128)(2,1)}), bf16[128,80,128]{2,1,0:T(8,128)(2,1)S(1)}, u32[]{:S(2)}, u32[]{:S(2)}) %all-to-all-start.2) | async-done | bytes 2621472 | tf_op jit(solution)/shard_map/all_to_all | solution.py:429
  84.8 5.6 %all-to-all-start.1 = ((bf16[128,80,128]{2,1,0:T(8,128)(2,1)}), bf16[128,80,128]{2,1,0:T(8,128)(2,1)}, u32[]{:S(2)}, u32[]{:S(2)}) async-start(bf16[128,80,128]{2,1,0:T(8,128)(2,1)} %get-tuple-element.34), calls=%async_computation.1 | async-start | bytes 5242880 | tf_op jit(solution)/shard_map/all_to_all | solution.py:429
  90.4 0.0 copy-done.19
  90.4 0.0 copy-done.20
  90.4 0.0 copy-done.17
  90.4 0.0 copy-done.18
  90.5 1.4 copy-done.15
  91.9 39.1 %near.2.old_ref = f32[33,16,256]{2,1,0:T(8,128)S(1)} custom-call(s32[2,384]{1,0:T(2,128)S(1)} %get-tuple-element.33.list_ref, bf16[128,80,128]{2,1,0:T(8,128)(2,1)S(1)} %all-to-all-done.2.got_ref, bf16[33,48,512]{2,1,0:T(8,128)(2,1)S(1)} %copy-done.15, f32[33,16,256]{2,1,0:T(8,128)S(1)} %get-tuple-element.36.old_ref), custom_call_target="tpu_custom_call", output_to_operand_aliasing={{}: (3, {})} | custom-call | flops 335544320 | bytes 8388608 | tf_op jit(solution)/shard_map/near/pallas_call | solution.py:430
  131.0 0.0 copy-start.6
  131.0 0.0 copy-start.9
  131.0 6.2 %all-to-all-done.1.got_ref = bf16[128,80,128]{2,1,0:T(8,128)(2,1)} async-done(((bf16[128,80,128]{2,1,0:T(8,128)(2,1)}), bf16[128,80,128]{2,1,0:T(8,128)(2,1)}, u32[]{:S(2)}, u32[]{:S(2)}) %all-to-all-start.1) | async-done | bytes 2621472 | tf_op jit(solution)/shard_map/all_to_all | solution.py:429
  137.2 1.4 copy-done.16
  138.6 7.5 %near.3.near_ref = f32[33,16,256]{2,1,0:T(8,128)S(1)} custom-call(s32[2,384]{1,0:T(2,128)S(1)} %get-tuple-element.33.list_ref, bf16[128,80,128]{2,1,0:T(8,128)(2,1)} %all-to-all-done.1.got_ref, bf16[33,48,512]{2,1,0:T(8,128)(2,1)S(1)} %copy-done.16, f32[33,16,256]{2,1,0:T(8,128)S(1)} %near.2.old_ref), custom_call_target="tpu_custom_call", output_to_operand_aliasing={{}: (3, {})} | custom-call | flops 335544320 | bytes 8388608 | tf_op jit(solution)/shard_map/near/pallas_call | solution.py:430
  146.1 0.0 copy-done.3
  146.1 0.0 copy-done.6
  146.1 0.0 copy-done.9
  146.1 0.0 copy-start
  146.1 3.7 %copy-done = bf16[2304,16,128]{2,1,0:T(8,128)(2,1)S(1)} copy-done((bf16[2304,16,128]{2,1,0:T(8,128)(2,1)S(1)}, bf16[2304,16,128]{2,1,0:T(8,128)(2,1)}, u32[]{:S(2)}) %copy-start) | copy-done | bytes 9437208
  149.8 3.1 %copy-done.1 = bf16[32,64,1728]{2,1,0:T(8,128)(2,1)S(1)} copy-done((bf16[32,64,1728]{2,1,0:T(8,128)(2,1)S(1)}, bf16[32,64,1728]{2,1,0:T(8,128)(2,1)}, u32[]{:S(2)}) %copy-start.1) | copy-done | bytes 7077912
  152.9 12.4 %far.1 = bf16[16,8192]{1,0:T(8,128)(2,1)} custom-call(s32[32,27]{1,0:T(8,128)S(1)} %multiply_add_fusion.code0_ref, s32[4,27]{1,0:T(4,128)S(1)} %add_add_fusion.code1_ref, bf16[2304,16,128]{2,1,0:T(8,128)(2,1)S(1)} %copy-done, bf16[32,64,1728]{2,1,0:T(8,128)(2,1)S(1)} %copy-done.1, bf16[4,64,1728]{2,1,0:T(8,128)(2,1)S(1)} %copy-done.9, ...), custom_call_target="tpu_custom_call" | custom-call | tf_op jit(solution)/shard_map/far/pallas_call | solution.py:445
  (16 shorter events, 0.1 us)
Async XLA Ops:
  6.5 139.5 %all-gather.2.cloned.1.call-start = ((), (), s32[]{:S(2)}) async-start(), calls=%async_computation.3 | async-start | bytes 9510912 | tf_op jit(solution)/shard_map/all_gather | solution.py:354
  6.5 1.2 copy-start.2
  7.8 0.9 copy-start.5
  8.7 0.9 copy-start.7
  9.7 17.1 %copy-start.8 = (bf16[16,8192]{1,0:T(8,128)(2,1)S(1)}, bf16[16,8192]{1,0:T(8,128)(2,1)}, u32[]{:S(2)}) copy-start(bf16[16,8192]{1,0:T(8,128)(2,1)} %x_ref.3) | copy-start | bytes 786436
  9.7 17.1 %copy-start.10 = (f32[8192]{0:T(1024)S(1)}, f32[8192]{0:T(1024)}, u32[]{:S(2)}) copy-start(f32[8192]{0:T(1024)} %param.15) | copy-start | bytes 98308
  11.0 0.7 copy-start.11
  11.7 0.7 copy-start.12
  13.3 21.1 %all-to-all-start = ((s32[128,1,128]{2,1,0:T(1,128)}), s32[128,1,128]{2,1,0:T(1,128)S(1)}, u32[]{:S(2)}, u32[]{:S(2)}) async-start(s32[128,1,128]{2,1,0:T(1,128)} %bitcast.3), calls=%async_computation | async-start | bytes 131072 | tf_op jit(solution)/shard_map/all_to_all | solution.py:367
  27.7 1.2 copy-start.13
  41.8 1.5 copy-start.4
  43.3 41.5 %all-to-all-start.2 = ((bf16[128,80,128]{2,1,0:T(8,128)(2,1)}), bf16[128,80,128]{2,1,0:T(8,128)(2,1)S(1)}, u32[]{:S(2)}, u32[]{:S(2)}) async-start(bf16[128,80,128]{2,1,0:T(8,128)(2,1)} %copy-done.4), calls=%async_computation.2 | async-start | bytes 5242880 | tf_op jit(solution)/shard_map/all_to_all | solution.py:429
  47.8 1.4 copy-start.14
  59.5 30.8 %copy-start.19 = (s32[4,27]{1,0:T(4,128)S(1)}, s32[4,27]{1,0:T(4,128)}, u32[]{:S(2)}) copy-start(s32[4,27]{1,0:T(4,128)} %param.23) | copy-start | bytes 1300
  59.5 30.8 %copy-start.20 = (s32[4,27]{1,0:T(4,128)S(1)}, s32[4,27]{1,0:T(4,128)}, u32[]{:S(2)}) copy-start(s32[4,27]{1,0:T(4,128)} %param.22) | copy-start | bytes 1300
  59.6 30.9 %copy-start.17 = (s32[32,27]{1,0:T(8,128)S(1)}, s32[32,27]{1,0:T(8,128)}, u32[]{:S(2)}) copy-start(s32[32,27]{1,0:T(8,128)} %param.21) | copy-start | bytes 10372
  59.6 30.9 %copy-start.18 = (s32[32,27]{1,0:T(8,128)S(1)}, s32[32,27]{1,0:T(8,128)}, u32[]{:S(2)}) copy-start(s32[32,27]{1,0:T(8,128)} %param.20) | copy-start | bytes 10372
  84.8 52.4 %all-to-all-start.1 = ((bf16[128,80,128]{2,1,0:T(8,128)(2,1)}), bf16[128,80,128]{2,1,0:T(8,128)(2,1)}, u32[]{:S(2)}, u32[]{:S(2)}) async-start(bf16[128,80,128]{2,1,0:T(8,128)(2,1)} %get-tuple-element.34), calls=%async_computation.1 | async-start | bytes 5242880 | tf_op jit(solution)/shard_map/all_to_all | solution.py:429
  90.4 1.4 copy-start.15
  131.0 15.1 %copy-start.3 = (bf16[32,64,256]{2,1,0:T(8,128)(2,1)S(1)}, bf16[32,64,256]{2,1,0:T(8,128)(2,1)}, u32[]{:S(2)}) copy-start(bf16[32,64,256]{2,1,0:T(8,128)(2,1)} %basis_ref.3) | copy-start | bytes 3145732
  131.0 15.1 %copy-start.6 = (bf16[4,64,512]{2,1,0:T(8,128)(2,1)S(1)}, bf16[4,64,512]{2,1,0:T(8,128)(2,1)}, u32[]{:S(2)}) copy-start(bf16[4,64,512]{2,1,0:T(8,128)(2,1)} %transfer_ref.3) | copy-start | bytes 786436
  131.0 15.1 %copy-start.9 = (bf16[4,64,1728]{2,1,0:T(8,128)(2,1)S(1)}, bf16[4,64,1728]{2,1,0:T(8,128)(2,1)}, u32[]{:S(2)}) copy-start(bf16[4,64,1728]{2,1,0:T(8,128)(2,1)} %couple1_ref.1) | copy-start | bytes 2654212
  137.2 1.4 copy-start.16
  146.1 3.7 %copy-start = (bf16[2304,16,128]{2,1,0:T(8,128)(2,1)S(1)}, bf16[2304,16,128]{2,1,0:T(8,128)(2,1)}, u32[]{:S(2)}) copy-start(bf16[2304,16,128]{2,1,0:T(8,128)(2,1)} %all-gather.2.cloned.1.call-done.table_ref) | copy-start | bytes 28311556
  149.8 3.1 %copy-start.1 = (bf16[32,64,1728]{2,1,0:T(8,128)(2,1)S(1)}, bf16[32,64,1728]{2,1,0:T(8,128)(2,1)}, u32[]{:S(2)}) copy-start(bf16[32,64,1728]{2,1,0:T(8,128)(2,1)} %couple0_ref.1) | copy-start | bytes 21233668
Sparse Core Ops, SparseCore 0:
  11.1 124.4 all-gather.1

commit v3 on v2

--- a/solution.py
+++ b/solution.py
@@ -44,6 +44,10 @@
     return high, low
 
 
+def shifted(number, by):
+    return lax.shift_right_logical(number, jnp.int32(by.bit_length() - 1))
+
+
 def contract_last(a, b):
     return lax.dot_general(a, b, (((1,), (1,)), ((), ())), preferred_element_type=jnp.float32)
 
@@ -52,30 +56,15 @@
     return pl.BlockSpec(memory_space=pltpu.VMEM)
 
 
+def hbm():
+    return pl.BlockSpec(memory_space=pltpu.HBM)
+
+
 def smem():
     return pl.BlockSpec(memory_space=pltpu.SMEM)
 
 
-def coef_kernel(x_ref, basis_ref, transfer_ref, out_ref):
-    boxes = basis_ref.shape[0]
-    parents = transfer_ref.shape[0]
-    leaf = []
-    for b in range(boxes):
-        c = contract_last(x_ref[:, b * LEAF : (b + 1) * LEAF], basis_ref[b])
-        leaf.append(c)
-        if b % 2:
-            out_ref[b // 2] = jnp.concatenate([leaf[b - 1], c], axis=1).astype(jnp.bfloat16)
-    up = []
-    for p in range(parents):
-        children = jnp.concatenate([out_ref[4 * p + i] for i in range(4)], axis=1)
-        up.append(contract_last(children, transfer_ref[p]))
-        if p % 2:
-            out_ref[boxes // 2 + p // 2] = jnp.concatenate([up[p - 1], up[p]], axis=1).astype(
-                jnp.bfloat16
-            )
-
-
-def plan_kernel(dev_ref, box_ref, asked_ref, place_ref):
+def plan(dev_ref, box_ref, asked_ref, place_ref):
     listed, count = dev_ref.shape
     devices = asked_ref.shape[0]
     owner = lax.broadcasted_iota(jnp.int32, (devices, count), 0)
@@ -107,6 +96,51 @@
     place_ref[...] = dev * SLOTS + jnp.concatenate(position, axis=0).astype(jnp.int32)
 
 
+def coefficients(x_ref, basis_ref, transfer_ref, out_ref, arrived):
+    boxes = basis_ref.shape[0]
+    parents = transfer_ref.shape[0]
+    leaf, up = [], []
+    for b in range(boxes):
+        if b % 8 == 0:
+            arrived(b // 8)
+        leaf.append(contract_last(x_ref[:, b * LEAF : (b + 1) * LEAF], basis_ref[b]))
+        if b % 2:
+            out_ref[b // 2] = jnp.concatenate(leaf[b - 1 :], axis=1).astype(jnp.bfloat16)
+    for p in range(parents):
+        children = jnp.concatenate([out_ref[4 * p + i] for i in range(4)], axis=1)
+        up.append(contract_last(children, transfer_ref[p]))
+        if p % 2:
+            out_ref[boxes // 2 + p // 2] = jnp.concatenate(up[p - 1 :], axis=1).astype(jnp.bfloat16)
+
+
+def first_kernel(
+    x_hbm, basis_hbm, transfer_hbm, dev_hbm, box_hbm, coef_ref, asked_ref, place_ref,
+    x_ref, basis_ref, transfer_ref, dev_ref, box_ref, sems,
+):
+    lists = [
+        pltpu.make_async_copy(dev_hbm, dev_ref, sems.at[0]),
+        pltpu.make_async_copy(box_hbm, box_ref, sems.at[1]),
+    ]
+    arrays = [
+        pltpu.make_async_copy(x_hbm, x_ref, sems.at[2]),
+        pltpu.make_async_copy(transfer_hbm, transfer_ref, sems.at[3]),
+    ]
+    eights = [
+        pltpu.make_async_copy(
+            basis_hbm.at[8 * i : 8 * i + 8], basis_ref.at[8 * i : 8 * i + 8], sems.at[4 + i]
+        )
+        for i in range(basis_ref.shape[0] // 8)
+    ]
+    for copy in lists + arrays + eights:
+        copy.start()
+    for copy in lists:
+        copy.wait()
+    plan(dev_ref, box_ref, asked_ref, place_ref)
+    for copy in arrays:
+        copy.wait()
+    coefficients(x_ref, basis_ref, transfer_ref, coef_ref, lambda i: eights[i].wait())
+
+
 def prepare_kernel(
     x_ref, weight_ref, source_ref, target_ref, table_ref, coded_ref, feature_ref
 ):
@@ -159,18 +193,20 @@
     block = out_refs[0].shape[0]
 
     def one(k, carry):
-        for d in (2 * k, 2 * k + 1):
+        for d in [4 * k + i for i in range(4)]:
             for part, out_ref in enumerate(out_refs):
                 coded = []
                 for p in range(PART):
                     q = asked_ref[step * block + d, part * PART + p]
-                    side = pl.multiple_of(q % PART * 32, 32)
-                    out_ref[d, 32 * p : 32 * (p + 1), :] = table_ref[q // PART, pl.ds(side, 32), :]
+                    side = pl.multiple_of((q & (PART - 1)) * 32, 32)
+                    out_ref[d, 32 * p : 32 * (p + 1), :] = table_ref[
+                        shifted(q, PART), pl.ds(side, 32), :
+                    ]
                     coded.append(coded_ref[q])
                 out_ref[d, 32 * PART :, :] = jnp.concatenate(coded, 0).astype(jnp.bfloat16)
         return carry
 
-    lax.fori_loop(0, block // 2, one, 0)
+    lax.fori_loop(0, block // 4, one, 0)
 
 
 def start_pair(entry, source_ref, feature_ref, square_ref, g):
@@ -247,7 +283,7 @@
 
     def entry(k):
         b = jnp.minimum(k, boxes - 1)
-        return b, b // PART, b % PART
+        return b, shifted(b, PART), b & (PART - 1)
 
     groups = boxes // (2 * GROUP)
     work(groups, entry, table_ref, feature_ref, total_ref, square_ref, kernel_ref)
@@ -258,7 +294,7 @@
         counts = list(counts)
         for i in range(listed):
             place = place_ref[i, b]
-            part = (place % SLOTS) // PART
+            part = shifted(place & (SLOTS - 1), PART)
             code = b * 1024 + place
             for c in range(parts):
                 list_ref[c, counts[c]] = code
@@ -277,43 +313,68 @@
 
     def entry(k):
         code = list_ref[part, k]
-        target, place = code // 1024, code % 1024
-        return target, place // SLOTS, place % PART
+        return shifted(code, 1024), shifted(code & 1023, SLOTS), code & (PART - 1)
 
     groups = list_ref[part, list_ref.shape[1] - 1]
     work(groups, entry, got_ref, feature_ref, total_ref, square_ref, kernel_ref)
 
 
 def far_kernel(
-    code0_ref, code1_ref, table_ref, couple0_ref, couple1_ref, transfer_ref, basis_ref, near_ref,
-    out_ref, stack_ref, up_ref,
+    code0_ref, code1_ref, table_hbm, couple0_hbm, couple1_ref, transfer_ref, basis_ref, near_ref,
+    out_ref, table_ref, couple0_ref, stack_ref, up_ref, sems,
 ):
     listed = code0_ref.shape[1]
+    parents = transfer_ref.shape[0]
     length = listed * WIDTH
     lane = lax.broadcasted_iota(jnp.int32, (SIDES, HALF), 1)
+    size = table_ref.shape[0] // 4
+    quarters = [
+        pltpu.make_async_copy(
+            table_hbm.at[i * size : (i + 1) * size],
+            table_ref.at[i * size : (i + 1) * size],
+            sems.at[i],
+        )
+        for i in range(4)
+    ]
+    eights = [
+        pltpu.make_async_copy(
+            couple0_hbm.at[8 * p : 8 * p + 8], couple0_ref.at[8 * p : 8 * p + 8], sems.at[4 + p]
+        )
+        for p in range(parents)
+    ]
+    for copy in quarters + eights:
+        copy.start()
+    for copy in quarters:
+        copy.wait()
 
     def piece(code_ref, row, j):
         code = code_ref[row, j]
-        tile = table_ref[code // 2]
-        return jnp.where((code + j) % 2 == 0, tile, pltpu.roll(tile, WIDTH, 1))
+        tile = table_ref[shifted(code, 2)]
+        return jnp.where(((code + j) & 1) == 0, tile, pltpu.roll(tile, WIDTH, 1))
 
     def gather(code_ref, row, into_ref, at):
         for j in range(0, listed, 2):
             tile = piece(code_ref, row, j)
             if j + 1 < listed:
                 tile = jnp.where(lane < WIDTH, tile, piece(code_ref, row, j + 1))
-            into_ref[pl.ds(at, SIDES), j * WIDTH : (j + 2) * WIDTH] = tile
-
-    def parent(p, carry):
-        gather(code1_ref, p, up_ref, 0)
+            into_ref[at : at + SIDES, j * WIDTH : (j + 2) * WIDTH] = tile
+
+    def gather_parent(p):
+        gather(code1_ref, p, up_ref.at[p % 2], 0)
         for i in range(8):
-            gather(code0_ref, 8 * p + i, stack_ref, i * SIDES)
-        parent_far = contract_last(up_ref[:, :length], couple1_ref[p]).astype(jnp.bfloat16)
+            gather(code0_ref, 8 * p + i, stack_ref.at[p % 2], i * SIDES)
+
+    gather_parent(0)
+    for p in range(parents):
+        eights[p].wait()
+        if p + 1 < parents:
+            gather_parent(p + 1)
+        parent_far = contract_last(up_ref[p % 2, :, :length], couple1_ref[p]).astype(jnp.bfloat16)
         down = jnp.dot(parent_far, transfer_ref[p], preferred_element_type=jnp.float32)
         for half in range(2):
             first = 8 * p + 4 * half
-            matrices = couple0_ref[pl.ds(first, 4)].reshape(4 * WIDTH, length)
-            stacked = stack_ref[4 * half * SIDES : 4 * (half + 1) * SIDES, :length]
+            matrices = couple0_ref[first : first + 4].reshape(4 * WIDTH, length)
+            stacked = stack_ref[p % 2, 4 * half * SIDES : 4 * (half + 1) * SIDES, :length]
             product = contract_last(stacked, matrices)
             for k in range(4):
                 i = 4 * half + k
@@ -322,11 +383,8 @@
                     + down[:, i * WIDTH : (i + 1) * WIDTH]
                 ).astype(jnp.bfloat16)
                 far = jnp.dot(field, basis_ref[first + k], preferred_element_type=jnp.float32)
-                at = pl.multiple_of((first + k) * LEAF, LEAF)
-                out_ref[:, pl.ds(at, LEAF)] = (far + near_ref[first + k]).astype(jnp.bfloat16)
-        return carry
-
-    lax.fori_loop(0, transfer_ref.shape[0], parent, 0)
+                at = (first + k) * LEAF
+                out_ref[:, at : at + LEAF] = (far + near_ref[first + k]).astype(jnp.bfloat16)
 
 
 def on_device(
@@ -343,27 +401,27 @@
 
     rows = boxes // 2 + parents // 2
 
-    coef = pl.pallas_call(
-        coef_kernel,
-        out_shape=jax.ShapeDtypeStruct((rows, SIDES, HALF), jnp.bfloat16),
-        in_specs=[vmem()] * 3,
-        out_specs=vmem(),
-        compiler_params=params(8),
-        name="coef",
-    )(x_values, basis, transfer)
-    table = lax.all_gather(coef, AXES, axis=0, tiled=True)
-
-    asked, place = pl.pallas_call(
-        plan_kernel,
+    coef, asked, place = pl.pallas_call(
+        first_kernel,
         out_shape=(
+            jax.ShapeDtypeStruct((rows, SIDES, HALF), jnp.bfloat16),
             jax.ShapeDtypeStruct((devices, devices), jnp.int32),
             jax.ShapeDtypeStruct((listed, boxes), jnp.int32),
         ),
-        in_specs=[vmem()] * 2,
-        out_specs=(vmem(), vmem()),
-        compiler_params=params(8),
-        name="plan",
-    )(near_partner_device.T, near_box.T)
+        in_specs=[hbm()] * 5,
+        out_specs=(vmem(), vmem(), vmem()),
+        scratch_shapes=[
+            pltpu.VMEM(x_values.shape, jnp.bfloat16),
+            pltpu.VMEM(basis.shape, jnp.bfloat16),
+            pltpu.VMEM(transfer.shape, jnp.bfloat16),
+            pltpu.VMEM((listed, boxes), jnp.int32),
+            pltpu.VMEM((listed, boxes), jnp.int32),
+            pltpu.SemaphoreType.DMA((4 + boxes // 8,)),
+        ],
+        compiler_params=params(60),
+        name="first",
+    )(x_values, basis, transfer, near_partner_device.T, near_box.T)
+    table = lax.all_gather(coef, AXES, axis=0, tiled=True)
     requests = lax.all_to_all(
         asked.reshape(devices, 1, devices), AXES, split_axis=0, concat_axis=0, tiled=True
     ).reshape(devices, devices)
@@ -404,7 +462,7 @@
             pl.BlockSpec((boxes, 8, HALF), lambda i: (0, 0, 0)),
         ],
         out_specs=[pl.BlockSpec((per_step, ROWS, HALF), lambda i: (i, 0, 0))] * parts,
-        compiler_params=params(8),
+        compiler_params=params(59),
         name="pack",
     )(requests, own, coded)
 
@@ -445,13 +503,16 @@
     return pl.pallas_call(
         far_kernel,
         out_shape=jax.ShapeDtypeStruct((SIDES, boxes * LEAF), jnp.bfloat16),
-        in_specs=[smem(), smem()] + [vmem()] * 6,
+        in_specs=[smem(), smem(), hbm(), hbm()] + [vmem()] * 4,
         out_specs=vmem(),
         scratch_shapes=[
-            pltpu.VMEM((8 * SIDES, padded), jnp.bfloat16),
-            pltpu.VMEM((SIDES, padded), jnp.bfloat16),
+            pltpu.VMEM(table.shape, jnp.bfloat16),
+            pltpu.VMEM(couple0.shape, jnp.bfloat16),
+            pltpu.VMEM((2, 8 * SIDES, padded), jnp.bfloat16),
+            pltpu.VMEM((2, SIDES, padded), jnp.bfloat16),
+            pltpu.SemaphoreType.DMA((4 + parents,)),
         ],
-        compiler_params=params(8),
+        compiler_params=params(56),
         name="far",
     )(
         first_far_partner_device * (2 * rows) + far0_box,

time: 173 us -> 165 us (0.954)
  local copies, waits for them, and re-layouts: 20.1 us -> 10.2 us
    unnamed x42 -> x32, local copies, waits for them, and re-layouts: 18.2 us -> 8.37 us
  transfers between devices with their start and end apart: 4 -> 4, of which waited for: 3 -> 3; matrix products, arithmetic and copies ran while one was open for 1% -> 2% of each run, Pallas kernels for 39% -> 38%
where the time goes in v3:
time: 165 us
  Pallas kernels  79.6 us (48%)
  waiting for transfers between devices  37.1 us (22%)
  starting transfers between devices  23.1 us (14%)
  between operations  13.6 us (8%)
  local copies, waits for them, and re-layouts  10.2 us (6%)
    pallas_call x2, Pallas kernels, on_device(): pl.pallas_call(functools.partial(near_kernel, part), out_shape=total_shap...  46.8 us
    all_to_all x2, waiting for transfers between devices, on_device(): lax.all_to_all(packed[part], AXES, split_axis=0, concat_axis=0, tiled=True)  33 us
    pallas_call x1, Pallas kernels, on_device(): pl.pallas_call(far_kernel, out_shape=jax.ShapeDtypeStruct((SIDES, boxes *...  13.4 us
    all_to_all x2, starting transfers between devices, on_device(): lax.all_to_all(packed[part], AXES, split_axis=0, concat_axis=0, tiled=True)  11.6 us
    all_to_all x1, starting transfers between devices, on_device(): lax.all_to_all(asked.reshape(devices, 1, devices), AXES, split_axis=0, co...  11.5 us
    pallas_call x1, Pallas kernels, on_device(): pl.pallas_call(own_kernel, out_shape=(total_shape, jax.ShapeDtypeStruct((...  8.85 us
    unnamed x32, local copies, waits for them, and re-layouts  8.37 us
    pallas_call x1, Pallas kernels, on_device(): pl.pallas_call(pack_kernel, out_shape=[jax.ShapeDtypeStruct((devices, ROW...  6.41 us
  transfers between devices with their start and end apart: 4, of which 3 were waited for; matrix products, arithmetic and copies ran while one was open for 2% of the time, Pallas kernels for 38%

profile of v3, /device:TPU:1, one launch (start us, length us, event | category | flops | bytes accessed | tf_op | source)
XLA Modules:
  0.0 164.8 jit_solution(16086235276230786397)
XLA Ops:
  6.5 0.0 copy-start
  6.5 0.0 copy-start.5
  6.5 0.0 all-gather.2.cloned.1.call-start
  6.5 3.1 %first.1 = (bf16[18,16,128]{2,1,0:T(8,128)(2,1)}, s32[128,128]{1,0:T(8,128)}, s32[8,32]{1,0:T(8,128)}) custom-call(bf16[16,8192]{1,0:T(8,128)(2,1)} %x_ref.1, bf16[32,64,256]{2,1,0:T(8,128)(2,1)} %basis_ref.1, bf16[4,64,512]{2,1,0:T(8,128)(2,1)} %transfer_ref.1, s32[8,32]{1,0:T(8,128)} %bitcast.20, s32[8,32]{1,0:T(8,128)} %bitcast.21), custom_call_target="tpu_custom_call" | custom-call | tf_op jit(solution)/shard_map/first/pallas_call | solution.py:404
  9.6 0.0 all-gather.2.cloned.1.call-update
  9.7 11.5 %all-to-all-start = ((s32[128,1,128]{2,1,0:T(1,128)}), s32[128,1,128]{2,1,0:T(1,128)S(1)}, u32[]{:S(2)}, u32[]{:S(2)}) async-start(s32[128,1,128]{2,1,0:T(1,128)} %bitcast.19), calls=%async_computation | async-start | bytes 131072 | tf_op jit(solution)/shard_map/all_to_all | solution.py:425
  21.2 0.9 pad.8
  22.1 0.9 pad_bitcast_fusion
  23.1 0.0 copy-done
  23.1 0.0 copy-done.5
  23.1 1.0 prepare.1
  24.1 0.0 copy-start.2
  24.1 0.7 copy-done.2
  24.8 0.0 copy-start.4
  24.8 0.7 copy-done.4
  25.5 0.0 copy-start.6
  25.5 1.2 copy-done.6
  26.7 4.1 %all-to-all-done = s32[128,1,128]{2,1,0:T(1,128)S(1)} async-done(((s32[128,1,128]{2,1,0:T(1,128)}), s32[128,1,128]{2,1,0:T(1,128)S(1)}, u32[]{:S(2)}, u32[]{:S(2)}) %all-to-all-start) | async-done | bytes 65568 | tf_op jit(solution)/shard_map/all_to_all | solution.py:425
  30.7 0.0 copy-start.11
  30.8 0.6 copy-done.11
  31.4 6.4 %pack.1 = (bf16[128,80,128]{2,1,0:T(8,128)(2,1)}, bf16[128,80,128]{2,1,0:T(8,128)(2,1)}) custom-call(s32[128,128]{1,0:T(8,128)} %bitcast.18, bf16[16,80,128]{2,1,0:T(8,128)(2,1)} %copy-done.2, f32[32,8,128]{2,1,0:T(8,128)} %copy-done.4), custom_call_target="tpu_custom_call" | custom-call | tf_op jit(solution)/shard_map/pack/pallas_call | solution.py:455
  37.8 0.0 copy-start.3
  37.8 0.0 copy-start.10
  37.8 5.7 %all-to-all-start.2 = ((bf16[128,80,128]{2,1,0:T(8,128)(2,1)}), bf16[128,80,128]{2,1,0:T(8,128)(2,1)S(1)}, u32[]{:S(2)}, u32[]{:S(2)}) async-start(bf16[128,80,128]{2,1,0:T(8,128)(2,1)} %get-tuple-element.37), calls=%async_computation.2 | async-start | bytes 5242880 | tf_op jit(solution)/shard_map/all_to_all | solution.py:487
  43.5 0.0 copy-done.3
  43.5 0.0 copy-done.10
  43.5 0.0 copy-start.7
  43.5 1.5 copy-done.7
  45.0 8.9 %own.1 = (f32[33,16,256]{2,1,0:T(8,128)S(1)}, s32[2,384]{1,0:T(2,128)S(1)}) custom-call(s32[8,32]{1,0:T(8,128)S(1)} %copy-done.10, bf16[16,80,128]{2,1,0:T(8,128)(2,1)S(1)} %copy-done.3, bf16[33,48,512]{2,1,0:T(8,128)(2,1)S(1)} %copy-done.7), custom_call_target="tpu_custom_call" | custom-call | flops 83886080 | bytes 4194304 | tf_op jit(solution)/shard_map/own/pallas_call | solution.py:471
  53.9 0.0 copy-start.14
  53.9 0.0 copy-start.15
  53.9 0.0 copy-start.12
  53.9 0.0 copy-start.13
  53.9 27.6 %all-to-all-done.2.got_ref = bf16[128,80,128]{2,1,0:T(8,128)(2,1)S(1)} async-done(((bf16[128,80,128]{2,1,0:T(8,128)(2,1)}), bf16[128,80,128]{2,1,0:T(8,128)(2,1)S(1)}, u32[]{:S(2)}, u32[]{:S(2)}) %all-to-all-start.2) | async-done | bytes 2621472 | tf_op jit(solution)/shard_map/all_to_all | solution.py:487
  81.6 5.9 %all-to-all-start.1 = ((bf16[128,80,128]{2,1,0:T(8,128)(2,1)}), bf16[128,80,128]{2,1,0:T(8,128)(2,1)}, u32[]{:S(2)}, u32[]{:S(2)}) async-start(bf16[128,80,128]{2,1,0:T(8,128)(2,1)} %get-tuple-element.36), calls=%async_computation.1 | async-start | bytes 5242880 | tf_op jit(solution)/shard_map/all_to_all | solution.py:487
  87.5 0.0 copy-done.14
  87.5 0.0 copy-done.15
  87.5 0.6 add_add_fusion.code1_ref
  88.1 0.0 copy-done.12
  88.1 0.0 copy-done.13
  88.1 0.6 multiply_add_fusion.code0_ref
  88.7 1.4 copy-done.8
  90.1 39.3 %near.2.old_ref = f32[33,16,256]{2,1,0:T(8,128)S(1)} custom-call(s32[2,384]{1,0:T(2,128)S(1)} %get-tuple-element.35.list_ref, bf16[128,80,128]{2,1,0:T(8,128)(2,1)S(1)} %all-to-all-done.2.got_ref, bf16[33,48,512]{2,1,0:T(8,128)(2,1)S(1)} %copy-done.8, f32[33,16,256]{2,1,0:T(8,128)S(1)} %get-tuple-element.38.old_ref), custom_call_target="tpu_custom_call", output_to_operand_aliasing={{}: (3, {})} | custom-call | flops 335544320 | bytes 8388608 | tf_op jit(solution)/shard_map/near/pallas_call | solution.py:488
  129.4 5.4 %all-to-all-done.1.got_ref = bf16[128,80,128]{2,1,0:T(8,128)(2,1)} async-done(((bf16[128,80,128]{2,1,0:T(8,128)(2,1)}), bf16[128,80,128]{2,1,0:T(8,128)(2,1)}, u32[]{:S(2)}, u32[]{:S(2)}) %all-to-all-start.1) | async-done | bytes 2621472 | tf_op jit(solution)/shard_map/all_to_all | solution.py:487
  134.8 1.4 copy-done.9
  136.2 7.6 %near.3.near_ref = f32[33,16,256]{2,1,0:T(8,128)S(1)} custom-call(s32[2,384]{1,0:T(2,128)S(1)} %get-tuple-element.35.list_ref, bf16[128,80,128]{2,1,0:T(8,128)(2,1)} %all-to-all-done.1.got_ref, bf16[33,48,512]{2,1,0:T(8,128)(2,1)S(1)} %copy-done.9, f32[33,16,256]{2,1,0:T(8,128)S(1)} %near.2.old_ref), custom_call_target="tpu_custom_call", output_to_operand_aliasing={{}: (3, {})} | custom-call | flops 335544320 | bytes 8388608 | tf_op jit(solution)/shard_map/near/pallas_call | solution.py:488
  143.7 0.8 copy-done.1
  144.5 13.4 %far.1 = bf16[16,8192]{1,0:T(8,128)(2,1)} custom-call(s32[32,27]{1,0:T(8,128)} %multiply_add_fusion.code0_ref, s32[4,27]{1,0:T(4,128)} %add_add_fusion.code1_ref, bf16[2304,16,128]{2,1,0:T(8,128)(2,1)} %all-gather.2.cloned.1.call-done.table_hbm, bf16[32,64,1728]{2,1,0:T(8,128)(2,1)} %couple0_hbm.1, bf16[4,64,1728]{2,1,0:T(8,128)(2,1)} %couple1_ref.1, ...), custom_call_target="tpu_custom_call" | custom-call | tf_op jit(solution)/shard_map/far/pallas_call | solution.py:503
  (5 shorter events, 0.1 us)
Async XLA Ops:
  6.5 16.6 %copy-start = (bf16[16,8192]{1,0:T(8,128)(2,1)S(1)}, bf16[16,8192]{1,0:T(8,128)(2,1)}, u32[]{:S(2)}) copy-start(bf16[16,8192]{1,0:T(8,128)(2,1)} %x_ref.1) | copy-start | bytes 786436
  6.5 16.6 %copy-start.5 = (f32[8192]{0:T(1024)S(1)}, f32[8192]{0:T(1024)}, u32[]{:S(2)}) copy-start(f32[8192]{0:T(1024)} %param.15) | copy-start | bytes 98308
  6.5 138.0 %all-gather.2.cloned.1.call-start = ((), (), s32[]{:S(2)}) async-start(), calls=%async_computation.3 | async-start | bytes 9510912 | tf_op jit(solution)/shard_map/all_gather | solution.py:424
  9.7 21.1 %all-to-all-start = ((s32[128,1,128]{2,1,0:T(1,128)}), s32[128,1,128]{2,1,0:T(1,128)S(1)}, u32[]{:S(2)}, u32[]{:S(2)}) async-start(s32[128,1,128]{2,1,0:T(1,128)} %bitcast.19), calls=%async_computation | async-start | bytes 131072 | tf_op jit(solution)/shard_map/all_to_all | solution.py:425
  24.1 0.7 copy-start.2
  24.8 0.7 copy-start.4
  25.5 1.2 copy-start.6
  30.7 0.6 copy-start.11
  37.8 5.7 %copy-start.3 = (bf16[16,80,128]{2,1,0:T(8,128)(2,1)S(1)}, bf16[16,80,128]{2,1,0:T(8,128)(2,1)}, u32[]{:S(2)}) copy-start(bf16[16,80,128]{2,1,0:T(8,128)(2,1)} %copy-done.2) | copy-start | bytes 983044
  37.8 5.7 %copy-start.10 = (s32[8,32]{1,0:T(8,128)S(1)}, s32[8,32]{1,0:T(8,128)}, u32[]{:S(2)}) copy-start(s32[8,32]{1,0:T(8,128)} %get-tuple-element.30.place_ref) | copy-start | bytes 3076
  37.8 43.8 %all-to-all-start.2 = ((bf16[128,80,128]{2,1,0:T(8,128)(2,1)}), bf16[128,80,128]{2,1,0:T(8,128)(2,1)S(1)}, u32[]{:S(2)}, u32[]{:S(2)}) async-start(bf16[128,80,128]{2,1,0:T(8,128)(2,1)} %get-tuple-element.37), calls=%async_computation.2 | async-start | bytes 5242880 | tf_op jit(solution)/shard_map/all_to_all | solution.py:487
  43.5 1.5 copy-start.7
  53.9 33.6 %copy-start.14 = (s32[4,27]{1,0:T(4,128)S(1)}, s32[4,27]{1,0:T(4,128)}, u32[]{:S(2)}) copy-start(s32[4,27]{1,0:T(4,128)} %param.23) | copy-start | bytes 1300
  53.9 33.6 %copy-start.15 = (s32[4,27]{1,0:T(4,128)S(1)}, s32[4,27]{1,0:T(4,128)}, u32[]{:S(2)}) copy-start(s32[4,27]{1,0:T(4,128)} %param.22) | copy-start | bytes 1300
  53.9 34.2 %copy-start.12 = (s32[32,27]{1,0:T(8,128)S(1)}, s32[32,27]{1,0:T(8,128)}, u32[]{:S(2)}) copy-start(s32[32,27]{1,0:T(8,128)} %param.21) | copy-start | bytes 10372
  53.9 34.2 %copy-start.13 = (s32[32,27]{1,0:T(8,128)S(1)}, s32[32,27]{1,0:T(8,128)}, u32[]{:S(2)}) copy-start(s32[32,27]{1,0:T(8,128)} %param.20) | copy-start | bytes 10372
  81.6 53.2 %all-to-all-start.1 = ((bf16[128,80,128]{2,1,0:T(8,128)(2,1)}), bf16[128,80,128]{2,1,0:T(8,128)(2,1)}, u32[]{:S(2)}, u32[]{:S(2)}) async-start(bf16[128,80,128]{2,1,0:T(8,128)(2,1)} %get-tuple-element.36), calls=%async_computation.1 | async-start | bytes 5242880 | tf_op jit(solution)/shard_map/all_to_all | solution.py:487
  88.7 1.4 copy-start.8
  134.8 1.4 copy-start.9
  143.7 0.8 copy-start.1
Sparse Core Ops, SparseCore 0:
  10.5 122.1 all-gather.1

commit v4 on v3

--- a/solution.py
+++ b/solution.py
@@ -188,22 +188,21 @@
     lax.fori_loop(0, boxes, one, 0)
 
 
-def pack_kernel(asked_ref, table_ref, coded_ref, *out_refs):
+def pack_kernel(part, asked_ref, table_ref, coded_ref, out_ref):
     step = pl.program_id(0)
-    block = out_refs[0].shape[0]
+    block = out_ref.shape[0]
 
     def one(k, carry):
         for d in [4 * k + i for i in range(4)]:
-            for part, out_ref in enumerate(out_refs):
-                coded = []
-                for p in range(PART):
-                    q = asked_ref[step * block + d, part * PART + p]
-                    side = pl.multiple_of((q & (PART - 1)) * 32, 32)
-                    out_ref[d, 32 * p : 32 * (p + 1), :] = table_ref[
-                        shifted(q, PART), pl.ds(side, 32), :
-                    ]
-                    coded.append(coded_ref[q])
-                out_ref[d, 32 * PART :, :] = jnp.concatenate(coded, 0).astype(jnp.bfloat16)
+            coded = []
+            for p in range(PART):
+                q = asked_ref[step * block + d, part * PART + p]
+                side = pl.multiple_of((q & (PART - 1)) * 32, 32)
+                out_ref[d, 32 * p : 32 * (p + 1), :] = table_ref[
+                    shifted(q, PART), pl.ds(side, 32), :
+                ]
+                coded.append(coded_ref[q])
+            out_ref[d, 32 * PART :, :] = jnp.concatenate(coded, 0).astype(jnp.bfloat16)
         return carry
 
     lax.fori_loop(0, block // 4, one, 0)
@@ -308,9 +307,7 @@
         list_ref[c, list_ref.shape[1] - 1] = (counts[c] + 2 * GROUP - 1) // (2 * GROUP)
 
 
-def near_kernel(part, list_ref, got_ref, feature_ref, old_ref, total_ref, square_ref, kernel_ref):
-    total_ref[...] = old_ref[...]
-
+def near_pairs(part, list_ref, got_ref, feature_ref, total_ref, square_ref, kernel_ref):
     def entry(k):
         code = list_ref[part, k]
         return shifted(code, 1024), shifted(code & 1023, SLOTS), code & (PART - 1)
@@ -319,32 +316,34 @@
     work(groups, entry, got_ref, feature_ref, total_ref, square_ref, kernel_ref)
 
 
-def far_kernel(
-    code0_ref, code1_ref, table_hbm, couple0_hbm, couple1_ref, transfer_ref, basis_ref, near_ref,
-    out_ref, table_ref, couple0_ref, stack_ref, up_ref, sems,
+def near_kernel(part, list_ref, got_ref, feature_ref, old_ref, total_ref, square_ref, kernel_ref):
+    total_ref[...] = old_ref[...]
+    near_pairs(part, list_ref, got_ref, feature_ref, total_ref, square_ref, kernel_ref)
+
+
+def last_kernel(
+    part, list_ref, code0_ref, code1_ref,
+    got_hbm, feature_hbm, old_hbm, table_hbm, couple0_hbm, couple1_hbm, transfer_hbm, basis_hbm,
+    out_ref,
+    got_ref, feature_ref, near_ref, table_ref, couple0_ref, couple1_ref, transfer_ref, basis_ref,
+    square_ref, kernel_ref, stack_ref, up_ref, sems,
 ):
     listed = code0_ref.shape[1]
     parents = transfer_ref.shape[0]
     length = listed * WIDTH
     lane = lax.broadcasted_iota(jnp.int32, (SIDES, HALF), 1)
-    size = table_ref.shape[0] // 4
-    quarters = [
-        pltpu.make_async_copy(
-            table_hbm.at[i * size : (i + 1) * size],
-            table_ref.at[i * size : (i + 1) * size],
-            sems.at[i],
-        )
-        for i in range(4)
+    pairs = [
+        (got_hbm, got_ref), (feature_hbm, feature_ref), (old_hbm, near_ref),
+        (table_hbm, table_ref), (transfer_hbm, transfer_ref), (couple1_hbm, couple1_ref),
+        (basis_hbm, basis_ref), (couple0_hbm, couple0_ref),
     ]
-    eights = [
-        pltpu.make_async_copy(
-            couple0_hbm.at[8 * p : 8 * p + 8], couple0_ref.at[8 * p : 8 * p + 8], sems.at[4 + p]
-        )
-        for p in range(parents)
-    ]
-    for copy in quarters + eights:
+    copies = [pltpu.make_async_copy(a, b, sems.at[i]) for i, (a, b) in enumerate(pairs)]
+    for copy in copies:
         copy.start()
-    for copy in quarters:
+    for copy in copies[:3]:
+        copy.wait()
+    near_pairs(part, list_ref, got_ref, feature_ref, near_ref, square_ref, kernel_ref)
+    for copy in copies[3:]:
         copy.wait()
 
     def piece(code_ref, row, j):
@@ -366,7 +365,6 @@
 
     gather_parent(0)
     for p in range(parents):
-        eights[p].wait()
         if p + 1 < parents:
             gather_parent(p + 1)
         parent_far = contract_last(up_ref[p % 2, :, :length], couple1_ref[p]).astype(jnp.bfloat16)
@@ -452,21 +450,25 @@
     parts = SLOTS // PART
     pairs = boxes * LEAF * LEAF
     per_step = 16
-    packed = pl.pallas_call(
-        pack_kernel,
-        out_shape=[jax.ShapeDtypeStruct((devices, ROWS, HALF), jnp.bfloat16)] * parts,
-        grid=(devices // per_step,),
-        in_specs=[
-            smem(),
-            pl.BlockSpec((boxes // PART, ROWS, HALF), lambda i: (0, 0, 0)),
-            pl.BlockSpec((boxes, 8, HALF), lambda i: (0, 0, 0)),
-        ],
-        out_specs=[pl.BlockSpec((per_step, ROWS, HALF), lambda i: (i, 0, 0))] * parts,
-        compiler_params=params(59),
-        name="pack",
-    )(requests, own, coded)
-
-    packed, own, features = lax.optimization_barrier((packed, own, features))
+
+    def pack(part):
+        return pl.pallas_call(
+            functools.partial(pack_kernel, part),
+            out_shape=jax.ShapeDtypeStruct((devices, ROWS, HALF), jnp.bfloat16),
+            grid=(devices // per_step,),
+            in_specs=[
+                smem(),
+                pl.BlockSpec((boxes // PART, ROWS, HALF), lambda i: (0, 0, 0)),
+                pl.BlockSpec((boxes, 8, HALF), lambda i: (0, 0, 0)),
+            ],
+            out_specs=pl.BlockSpec((per_step, ROWS, HALF), lambda i: (i, 0, 0)),
+            compiler_params=params(59),
+            name="pack",
+        )(requests, own, coded)
+
+    packed = [pack(0)]
+    packed[0], requests, place = lax.optimization_barrier((packed[0], requests, place))
+    packed += [pack(part) for part in range(1, parts)]
     total_shape = jax.ShapeDtypeStruct((boxes + 1, SIDES, LEAF), jnp.float32)
     near, listing = pl.pallas_call(
         own_kernel,
@@ -480,11 +482,13 @@
         ),
         name="own",
     )(place, own, features)
-    later, near, listing = lax.optimization_barrier((packed[1:], near, listing))
+    later, listing = lax.optimization_barrier((packed[1:], listing))
     packed = [packed[0], *later]
 
     for part in range(parts):
         got = lax.all_to_all(packed[part], AXES, split_axis=0, concat_axis=0, tiled=True)
+        if part == parts - 1:
+            break
         near = pl.pallas_call(
             functools.partial(near_kernel, part),
             out_shape=total_shape,
@@ -500,24 +504,26 @@
         )(listing, got, features, near)
 
     padded = (couple0.shape[2] + HALF - 1) // HALF * HALF
+    held = [got, features, near, table, couple0, couple1, transfer, basis]
     return pl.pallas_call(
-        far_kernel,
+        functools.partial(last_kernel, parts - 1),
         out_shape=jax.ShapeDtypeStruct((SIDES, boxes * LEAF), jnp.bfloat16),
-        in_specs=[smem(), smem(), hbm(), hbm()] + [vmem()] * 4,
+        in_specs=[smem()] * 3 + [hbm()] * len(held),
         out_specs=vmem(),
-        scratch_shapes=[
-            pltpu.VMEM(table.shape, jnp.bfloat16),
-            pltpu.VMEM(couple0.shape, jnp.bfloat16),
+        scratch_shapes=[pltpu.VMEM(a.shape, a.dtype) for a in held]
+        + scratch
+        + [
             pltpu.VMEM((2, 8 * SIDES, padded), jnp.bfloat16),
             pltpu.VMEM((2, SIDES, padded), jnp.bfloat16),
-            pltpu.SemaphoreType.DMA((4 + parents,)),
+            pltpu.SemaphoreType.DMA((len(held),)),
         ],
-        compiler_params=params(56),
-        name="far",
+        compiler_params=params(59),
+        name="last",
     )(
+        listing,
         first_far_partner_device * (2 * rows) + far0_box,
         far1_dev * (2 * rows) + boxes + far1_box,
-        table, couple0, couple1, transfer, basis, near,
+        *held,
     )
 
 

time: 165 us -> 156 us (0.945)
  waiting for transfers between devices: 37.1 us -> 32.3 us
  local copies, waits for them, and re-layouts: 10.2 us -> 7.34 us
    pallas_call x2 -> x1, Pallas kernels: 46.8 us -> 39.3 us  [on_device(): pl.pallas_call(functools.partial(near_kernel, part), out_shape=total_shap...]
    pallas_call x2 -> x3, Pallas kernels: 19.8 us -> 26.2 us  [the longest x1 15.2 us: on_device(): pl.pallas_call(functools.partial(last_kernel, parts - 1), out_shape=jax.S...]
    all_to_all x2, waiting for transfers between devices: 33 us -> 28.2 us  [on_device(): lax.all_to_all(packed[part], AXES, split_axis=0, concat_axis=0, tiled=True)]
    unnamed x32, local copies, waits for them, and re-layouts: 8.37 us -> 5.48 us
  transfers between devices with their start and end apart: 4 -> 4, of which waited for: 3 -> 3; matrix products, arithmetic and copies ran while one was open for 2% -> 2% of each run, Pallas kernels for 38% -> 39%
where the time goes in v4:
time: 156 us
  Pallas kernels  78.4 us (50%)
  waiting for transfers between devices  32.3 us (21%)
  starting transfers between devices  22.9 us (15%)
  between operations  13.6 us (9%)
  local copies, waits for them, and re-layouts  7.34 us (5%)
    pallas_call x1, Pallas kernels, on_device(): pl.pallas_call(functools.partial(near_kernel, part), out_shape=total_shap...  39.3 us
    all_to_all x2, waiting for transfers between devices, on_device(): lax.all_to_all(packed[part], AXES, split_axis=0, concat_axis=0, tiled=True)  28.2 us
    pallas_call x1, Pallas kernels, on_device(): pl.pallas_call(functools.partial(last_kernel, parts - 1), out_shape=jax.S...  15.2 us
    all_to_all x1, starting transfers between devices, on_device(): lax.all_to_all(asked.reshape(devices, 1, devices), AXES, split_axis=0, co...  11.5 us
    all_to_all x2, starting transfers between devices, on_device(): lax.all_to_all(packed[part], AXES, split_axis=0, concat_axis=0, tiled=True)  11.4 us
    pallas_call x2, Pallas kernels, pack(): pl.pallas_call(functools.partial(pack_kernel, part), out_shape=jax.ShapeD...  11 us
    pallas_call x1, Pallas kernels, on_device(): pl.pallas_call(own_kernel, out_shape=(total_shape, jax.ShapeDtypeStruct((...  8.83 us
    unnamed x32, local copies, waits for them, and re-layouts  5.48 us
  transfers between devices with their start and end apart: 4, of which 3 were waited for; matrix products, arithmetic and copies ran while one was open for 2% of the time, Pallas kernels for 39%

profile of v4, /device:TPU:1, one launch (start us, length us, event | category | flops | bytes accessed | tf_op | source)
XLA Modules:
  0.0 155.7 jit_solution(2383924661980893791)
XLA Ops:
  6.5 0.0 copy-start.5
  6.5 0.0 copy-start.8
  6.5 0.0 all-gather.2.cloned.1.call-start
  6.5 3.1 %first.1 = (bf16[18,16,128]{2,1,0:T(8,128)(2,1)}, s32[128,128]{1,0:T(8,128)}, s32[8,32]{1,0:T(8,128)}) custom-call(bf16[16,8192]{1,0:T(8,128)(2,1)} %x_ref.1, bf16[32,64,256]{2,1,0:T(8,128)(2,1)} %basis_hbm.3, bf16[4,64,512]{2,1,0:T(8,128)(2,1)} %transfer_hbm.3, s32[8,32]{1,0:T(8,128)} %bitcast.21, s32[8,32]{1,0:T(8,128)} %bitcast.22), custom_call_target="tpu_custom_call" | custom-call | tf_op jit(solution)/shard_map/first/pallas_call | solution.py:402
  9.6 0.0 all-gather.2.cloned.1.call-update
  9.7 11.5 %all-to-all-start = ((s32[128,1,128]{2,1,0:T(1,128)}), s32[128,1,128]{2,1,0:T(1,128)S(1)}, u32[]{:S(2)}, u32[]{:S(2)}) async-start(s32[128,1,128]{2,1,0:T(1,128)} %bitcast.20), calls=%async_computation | async-start | bytes 131072 | tf_op jit(solution)/shard_map/all_to_all | solution.py:423
  21.2 0.9 pad.8
  22.1 0.9 pad_bitcast_fusion
  23.1 0.0 copy-done.5
  23.1 0.0 copy-done.8
  23.1 1.0 prepare.1
  24.1 0.0 copy-start
  24.1 1.2 copy-done
  25.3 0.0 copy-start.3
  25.3 0.7 copy-done.3
  26.0 0.0 copy-start.7
  26.0 0.7 copy-done.7
  26.7 4.1 %all-to-all-done = s32[128,1,128]{2,1,0:T(1,128)S(1)} async-done(((s32[128,1,128]{2,1,0:T(1,128)}), s32[128,1,128]{2,1,0:T(1,128)S(1)}, u32[]{:S(2)}, u32[]{:S(2)}) %all-to-all-start) | async-done | bytes 65568 | tf_op jit(solution)/shard_map/all_to_all | solution.py:423
  30.7 0.6 copy-done.11
  31.4 5.4 %pack.2 = bf16[128,80,128]{2,1,0:T(8,128)(2,1)} custom-call(s32[128,128]{1,0:T(8,128)} %bitcast.16, bf16[16,80,128]{2,1,0:T(8,128)(2,1)} %copy-done.3, f32[32,8,128]{2,1,0:T(8,128)} %copy-done.7), custom_call_target="tpu_custom_call" | custom-call | tf_op jit(solution)/shard_map/pack/pallas_call | solution.py:455
  36.8 5.7 %all-to-all-start.2 = ((bf16[128,80,128]{2,1,0:T(8,128)(2,1)}), bf16[128,80,128]{2,1,0:T(8,128)(2,1)S(1)}, u32[]{:S(2)}, u32[]{:S(2)}) async-start(bf16[128,80,128]{2,1,0:T(8,128)(2,1)} %pack.2), calls=%async_computation.2 | async-start | bytes 5242880 | tf_op jit(solution)/shard_map/all_to_all | solution.py:489
  42.5 0.0 copy-start.1
  42.5 0.0 copy-start.4
  42.5 0.0 copy-start.10
  42.5 5.6 %pack.3 = bf16[128,80,128]{2,1,0:T(8,128)(2,1)} custom-call(s32[128,128]{1,0:T(8,128)} %bitcast.17, bf16[16,80,128]{2,1,0:T(8,128)(2,1)} %copy-done.3, f32[32,8,128]{2,1,0:T(8,128)} %copy-done.7), custom_call_target="tpu_custom_call" | custom-call | tf_op jit(solution)/shard_map/pack/pallas_call | solution.py:455
  48.1 0.0 copy-done.1
  48.1 0.0 copy-done.4
  48.1 0.0 copy-done.10
  48.1 8.8 %own.1 = (f32[33,16,256]{2,1,0:T(8,128)S(1)}, s32[2,384]{1,0:T(2,128)S(1)}) custom-call(s32[8,32]{1,0:T(8,128)S(1)} %copy-done.10, bf16[16,80,128]{2,1,0:T(8,128)(2,1)S(1)} %copy-done.4, bf16[33,48,512]{2,1,0:T(8,128)(2,1)S(1)} %copy-done.1), custom_call_target="tpu_custom_call" | custom-call | flops 83886080 | bytes 4194304 | tf_op jit(solution)/shard_map/own/pallas_call | solution.py:473
  56.9 0.0 copy-start.9
  57.0 0.0 copy-start.14
  57.0 0.0 copy-start.15
  57.0 0.0 copy-start.12
  57.0 0.0 copy-start.13
  57.0 23.5 %all-to-all-done.2.got_ref = bf16[128,80,128]{2,1,0:T(8,128)(2,1)S(1)} async-done(((bf16[128,80,128]{2,1,0:T(8,128)(2,1)}), bf16[128,80,128]{2,1,0:T(8,128)(2,1)S(1)}, u32[]{:S(2)}, u32[]{:S(2)}) %all-to-all-start.2) | async-done | bytes 2621472 | tf_op jit(solution)/shard_map/all_to_all | solution.py:489
  80.5 5.7 %all-to-all-start.1 = ((bf16[128,80,128]{2,1,0:T(8,128)(2,1)}), bf16[128,80,128]{2,1,0:T(8,128)(2,1)}, u32[]{:S(2)}, u32[]{:S(2)}) async-start(bf16[128,80,128]{2,1,0:T(8,128)(2,1)} %pack.3), calls=%async_computation.1 | async-start | bytes 5242880 | tf_op jit(solution)/shard_map/all_to_all | solution.py:489
  86.2 0.0 copy-done.14
  86.2 0.0 copy-done.15
  86.2 0.6 add_add_fusion.code1_ref
  86.8 0.0 copy-done.12
  86.8 0.0 copy-done.13
  86.8 0.6 multiply_add_fusion.code0_ref
  87.4 0.0 copy-done.9
  87.4 1.4 copy-done.2
  88.8 39.3 %near.1.old_hbm = f32[33,16,256]{2,1,0:T(8,128)S(1)} custom-call(s32[2,384]{1,0:T(2,128)S(1)} %get-tuple-element.26.list_ref, bf16[128,80,128]{2,1,0:T(8,128)(2,1)S(1)} %all-to-all-done.2.got_ref, bf16[33,48,512]{2,1,0:T(8,128)(2,1)S(1)} %copy-done.2, f32[33,16,256]{2,1,0:T(8,128)S(1)} %get-tuple-element.29.old_ref), custom_call_target="tpu_custom_call", output_to_operand_aliasing={{}: (3, {})} | custom-call | flops 335544320 | bytes 8388608 | tf_op jit(solution)/shard_map/near/pallas_call | solution.py:492
  128.1 0.8 copy-done.6
  128.9 4.7 %all-to-all-done.1.got_hbm = bf16[128,80,128]{2,1,0:T(8,128)(2,1)} async-done(((bf16[128,80,128]{2,1,0:T(8,128)(2,1)}), bf16[128,80,128]{2,1,0:T(8,128)(2,1)}, u32[]{:S(2)}, u32[]{:S(2)}) %all-to-all-start.1) | async-done | bytes 2621472 | tf_op jit(solution)/shard_map/all_to_all | solution.py:489
  133.6 15.2 %last.1 = bf16[16,8192]{1,0:T(8,128)(2,1)} custom-call(s32[2,384]{1,0:T(2,128)} %copy-done.9, s32[32,27]{1,0:T(8,128)} %multiply_add_fusion.code0_ref, s32[4,27]{1,0:T(4,128)} %add_add_fusion.code1_ref, bf16[128,80,128]{2,1,0:T(8,128)(2,1)} %all-to-all-done.1.got_hbm, bf16[33,48,512]{2,1,0:T(8,128)(2,1)} %copy-done, f32[33,16,256]{2,1,0:T(8,128)} %copy-done.6, ...), custom_call_target="tpu_custom_call" | custom-call | tf_op jit(solution)/shard_map/last/pallas_call | solution.py:508
  (5 shorter events, 0.1 us)
Async XLA Ops:
  6.5 16.6 %copy-start.5 = (bf16[16,8192]{1,0:T(8,128)(2,1)S(1)}, bf16[16,8192]{1,0:T(8,128)(2,1)}, u32[]{:S(2)}) copy-start(bf16[16,8192]{1,0:T(8,128)(2,1)} %x_ref.1) | copy-start | bytes 786436
  6.5 16.6 %copy-start.8 = (f32[8192]{0:T(1024)S(1)}, f32[8192]{0:T(1024)}, u32[]{:S(2)}) copy-start(f32[8192]{0:T(1024)} %param.15) | copy-start | bytes 98308
  6.5 127.1 %all-gather.2.cloned.1.call-start = ((), (), s32[]{:S(2)}) async-start(), calls=%async_computation.3 | async-start | bytes 9510912 | tf_op jit(solution)/shard_map/all_gather | solution.py:422
  9.7 21.1 %all-to-all-start = ((s32[128,1,128]{2,1,0:T(1,128)}), s32[128,1,128]{2,1,0:T(1,128)S(1)}, u32[]{:S(2)}, u32[]{:S(2)}) async-start(s32[128,1,128]{2,1,0:T(1,128)} %bitcast.20), calls=%async_computation | async-start | bytes 131072 | tf_op jit(solution)/shard_map/all_to_all | solution.py:423
  24.1 1.2 copy-start
  25.3 0.7 copy-start.3
  26.0 0.7 copy-start.7
  30.7 0.6 copy-start.11
  36.8 43.7 %all-to-all-start.2 = ((bf16[128,80,128]{2,1,0:T(8,128)(2,1)}), bf16[128,80,128]{2,1,0:T(8,128)(2,1)S(1)}, u32[]{:S(2)}, u32[]{:S(2)}) async-start(bf16[128,80,128]{2,1,0:T(8,128)(2,1)} %pack.2), calls=%async_computation.2 | async-start | bytes 5242880 | tf_op jit(solution)/shard_map/all_to_all | solution.py:489
  42.5 5.6 %copy-start.1 = (bf16[33,48,512]{2,1,0:T(8,128)(2,1)S(1)}, bf16[33,48,512]{2,1,0:T(8,128)(2,1)}, u32[]{:S(2)}) copy-start(bf16[33,48,512]{2,1,0:T(8,128)(2,1)} %copy-done) | copy-start | bytes 4866052
  42.5 5.6 %copy-start.4 = (bf16[16,80,128]{2,1,0:T(8,128)(2,1)S(1)}, bf16[16,80,128]{2,1,0:T(8,128)(2,1)}, u32[]{:S(2)}) copy-start(bf16[16,80,128]{2,1,0:T(8,128)(2,1)} %copy-done.3) | copy-start | bytes 983044
  42.5 5.6 %copy-start.10 = (s32[8,32]{1,0:T(8,128)S(1)}, s32[8,32]{1,0:T(8,128)}, u32[]{:S(2)}) copy-start(s32[8,32]{1,0:T(8,128)} %get-tuple-element.23.place_ref) | copy-start | bytes 3076
  56.9 30.4 %copy-start.9 = (s32[2,384]{1,0:T(2,128)}, s32[2,384]{1,0:T(2,128)S(1)}, u32[]{:S(2)}) copy-start(s32[2,384]{1,0:T(2,128)S(1)} %get-tuple-element.26.list_ref) | copy-start | bytes 9220
  57.0 29.2 %copy-start.14 = (s32[4,27]{1,0:T(4,128)S(1)}, s32[4,27]{1,0:T(4,128)}, u32[]{:S(2)}) copy-start(s32[4,27]{1,0:T(4,128)} %param.23) | copy-start | bytes 1300
  57.0 29.2 %copy-start.15 = (s32[4,27]{1,0:T(4,128)S(1)}, s32[4,27]{1,0:T(4,128)}, u32[]{:S(2)}) copy-start(s32[4,27]{1,0:T(4,128)} %param.22) | copy-start | bytes 1300
  57.0 29.8 %copy-start.12 = (s32[32,27]{1,0:T(8,128)S(1)}, s32[32,27]{1,0:T(8,128)}, u32[]{:S(2)}) copy-start(s32[32,27]{1,0:T(8,128)} %param.21) | copy-start | bytes 10372
  57.0 29.8 %copy-start.13 = (s32[32,27]{1,0:T(8,128)S(1)}, s32[32,27]{1,0:T(8,128)}, u32[]{:S(2)}) copy-start(s32[32,27]{1,0:T(8,128)} %param.20) | copy-start | bytes 10372
  80.5 53.1 %all-to-all-start.1 = ((bf16[128,80,128]{2,1,0:T(8,128)(2,1)}), bf16[128,80,128]{2,1,0:T(8,128)(2,1)}, u32[]{:S(2)}, u32[]{:S(2)}) async-start(bf16[128,80,128]{2,1,0:T(8,128)(2,1)} %pack.3), calls=%async_computation.1 | async-start | bytes 5242880 | tf_op jit(solution)/shard_map/all_to_all | solution.py:489
  87.4 1.4 copy-start.2
  128.1 0.8 copy-start.6
Sparse Core Ops, SparseCore 0:
  10.5 121.0 all-gather.1

commit v5 on v4

--- a/solution.py
+++ b/solution.py
@@ -338,10 +338,12 @@
         (basis_hbm, basis_ref), (couple0_hbm, couple0_ref),
     ]
     copies = [pltpu.make_async_copy(a, b, sems.at[i]) for i, (a, b) in enumerate(pairs)]
-    for copy in copies:
+    for copy in copies[:3]:
         copy.start()
     for copy in copies[:3]:
         copy.wait()
+    for copy in copies[3:]:
+        copy.start()
     near_pairs(part, list_ref, got_ref, feature_ref, near_ref, square_ref, kernel_ref)
     for copy in copies[3:]:
         copy.wait()
@@ -449,7 +451,7 @@
     ]
     parts = SLOTS // PART
     pairs = boxes * LEAF * LEAF
-    per_step = 16
+    per_step = devices // 2
 
     def pack(part):
         return pl.pallas_call(
@@ -482,7 +484,11 @@
         ),
         name="own",
     )(place, own, features)
-    later, listing = lax.optimization_barrier((packed[1:], listing))
+    codes = (
+        first_far_partner_device * (2 * rows) + far0_box,
+        far1_dev * (2 * rows) + boxes + far1_box,
+    )
+    later, listing, codes = lax.optimization_barrier((packed[1:], listing, codes))
     packed = [packed[0], *later]
 
     for part in range(parts):
@@ -521,8 +527,7 @@
         name="last",
     )(
         listing,
-        first_far_partner_device * (2 * rows) + far0_box,
-        far1_dev * (2 * rows) + boxes + far1_box,
+        *codes,
         *held,
     )
 

time: 156 us -> 155 us (level)
  Pallas kernels: 78.4 us -> 76 us
    pallas_call x2, Pallas kernels: 11 us -> 7.83 us  [pack(): pl.pallas_call(functools.partial(pack_kernel, part), out_shape=jax.ShapeD...]
  transfers between devices with their start and end apart: 4 -> 4, of which waited for: 3 -> 3; matrix products, arithmetic and copies ran while one was open for 2% -> 2% of each run, Pallas kernels for 39% -> 37%
where the time goes in v5:
time: 155 us
  Pallas kernels  76 us (49%)
  waiting for transfers between devices  33.4 us (22%)
  starting transfers between devices  22.8 us (15%)
  between operations  13.6 us (9%)
  local copies, waits for them, and re-layouts  7.74 us (5%)
    pallas_call x1, Pallas kernels, on_device(): pl.pallas_call(functools.partial(near_kernel, part), out_shape=total_shap...  39.3 us
    all_to_all x2, waiting for transfers between devices, on_device(): lax.all_to_all(packed[part], AXES, split_axis=0, concat_axis=0, tiled=True)  29.3 us
    pallas_call x1, Pallas kernels, on_device(): pl.pallas_call(functools.partial(last_kernel, parts - 1), out_shape=jax.S...  16 us
    all_to_all x1, starting transfers between devices, on_device(): lax.all_to_all(asked.reshape(devices, 1, devices), AXES, split_axis=0, co...  11.5 us
    all_to_all x2, starting transfers between devices, on_device(): lax.all_to_all(packed[part], AXES, split_axis=0, concat_axis=0, tiled=True)  11.3 us
    pallas_call x1, Pallas kernels, on_device(): pl.pallas_call(own_kernel, out_shape=(total_shape, jax.ShapeDtypeStruct((...  8.83 us
    pallas_call x2, Pallas kernels, pack(): pl.pallas_call(functools.partial(pack_kernel, part), out_shape=jax.ShapeD...  7.83 us
    unnamed x32, local copies, waits for them, and re-layouts  5.87 us
  transfers between devices with their start and end apart: 4, of which 3 were waited for; matrix products, arithmetic and copies ran while one was open for 2% of the time, Pallas kernels for 37%

profile of v5, /device:TPU:1, one launch (start us, length us, event | category | flops | bytes accessed | tf_op | source)
XLA Modules:
  0.0 154.7 jit_solution(8064520344500849306)
XLA Ops:
  6.5 0.0 copy-start.5
  6.5 0.0 copy-start.8
  6.5 0.0 all-gather.2.cloned.1.call-start
  6.5 3.1 %first.1 = (bf16[18,16,128]{2,1,0:T(8,128)(2,1)}, s32[128,128]{1,0:T(8,128)}, s32[8,32]{1,0:T(8,128)}) custom-call(bf16[16,8192]{1,0:T(8,128)(2,1)} %x_ref.1, bf16[32,64,256]{2,1,0:T(8,128)(2,1)} %basis_hbm.3, bf16[4,64,512]{2,1,0:T(8,128)(2,1)} %transfer_hbm.3, s32[8,32]{1,0:T(8,128)} %bitcast.21, s32[8,32]{1,0:T(8,128)} %bitcast.22), custom_call_target="tpu_custom_call" | custom-call | tf_op jit(solution)/shard_map/first/pallas_call | solution.py:404
  9.6 0.0 all-gather.2.cloned.1.call-update
  9.7 11.5 %all-to-all-start = ((s32[128,1,128]{2,1,0:T(1,128)}), s32[128,1,128]{2,1,0:T(1,128)S(1)}, u32[]{:S(2)}, u32[]{:S(2)}) async-start(s32[128,1,128]{2,1,0:T(1,128)} %bitcast.20), calls=%async_computation | async-start | bytes 131072 | tf_op jit(solution)/shard_map/all_to_all | solution.py:425
  21.2 0.9 pad.8
  22.1 0.9 pad_bitcast_fusion
  23.1 0.0 copy-done.5
  23.1 0.0 copy-done.8
  23.1 1.0 prepare.1
  24.1 0.0 copy-start
  24.1 1.2 copy-done
  25.3 0.0 copy-start.3
  25.3 0.7 copy-done.3
  26.0 0.0 copy-start.7
  26.0 0.7 copy-done.7
  26.7 4.1 %all-to-all-done = s32[128,1,128]{2,1,0:T(1,128)S(1)} async-done(((s32[128,1,128]{2,1,0:T(1,128)}), s32[128,1,128]{2,1,0:T(1,128)S(1)}, u32[]{:S(2)}, u32[]{:S(2)}) %all-to-all-start) | async-done | bytes 65568 | tf_op jit(solution)/shard_map/all_to_all | solution.py:425
  30.7 0.0 copy-start.11
  30.7 0.6 copy-done.11
  31.4 3.9 %pack.2 = bf16[128,80,128]{2,1,0:T(8,128)(2,1)} custom-call(s32[128,128]{1,0:T(8,128)} %bitcast.16, bf16[16,80,128]{2,1,0:T(8,128)(2,1)} %copy-done.3, f32[32,8,128]{2,1,0:T(8,128)} %copy-done.7), custom_call_target="tpu_custom_call" | custom-call | tf_op jit(solution)/shard_map/pack/pallas_call | solution.py:457
  35.3 0.0 copy-start.15
  35.3 0.0 copy-start.13
  35.3 5.7 %all-to-all-start.2 = ((bf16[128,80,128]{2,1,0:T(8,128)(2,1)}), bf16[128,80,128]{2,1,0:T(8,128)(2,1)S(1)}, u32[]{:S(2)}, u32[]{:S(2)}) async-start(bf16[128,80,128]{2,1,0:T(8,128)(2,1)} %pack.2), calls=%async_computation.2 | async-start | bytes 5242880 | tf_op jit(solution)/shard_map/all_to_all | solution.py:495
  41.0 0.0 copy-done.14
  41.0 0.0 copy-done.15
  41.0 0.0 copy-start.1
  41.0 0.0 copy-start.4
  41.0 0.0 copy-start.10
  41.1 0.6 add_add_fusion.code1_ref
  41.6 0.0 copy-done.12
  41.6 0.0 copy-done.13
  41.6 0.6 multiply_add_fusion.code0_ref
  42.3 3.9 %pack.3 = bf16[128,80,128]{2,1,0:T(8,128)(2,1)} custom-call(s32[128,128]{1,0:T(8,128)} %bitcast.17, bf16[16,80,128]{2,1,0:T(8,128)(2,1)} %copy-done.3, f32[32,8,128]{2,1,0:T(8,128)} %copy-done.7), custom_call_target="tpu_custom_call" | custom-call | tf_op jit(solution)/shard_map/pack/pallas_call | solution.py:457
  46.2 0.0 copy-done.1
  46.2 0.0 copy-done.4
  46.2 0.0 copy-done.10
  46.2 8.8 %own.1 = (f32[33,16,256]{2,1,0:T(8,128)S(1)}, s32[2,384]{1,0:T(2,128)S(1)}) custom-call(s32[8,32]{1,0:T(8,128)S(1)} %copy-done.10, bf16[16,80,128]{2,1,0:T(8,128)(2,1)S(1)} %copy-done.4, bf16[33,48,512]{2,1,0:T(8,128)(2,1)S(1)} %copy-done.1), custom_call_target="tpu_custom_call" | custom-call | flops 83886080 | bytes 4194304 | tf_op jit(solution)/shard_map/own/pallas_call | solution.py:475
  55.0 0.0 copy-start.9
  55.0 24.0 %all-to-all-done.2.got_ref = bf16[128,80,128]{2,1,0:T(8,128)(2,1)S(1)} async-done(((bf16[128,80,128]{2,1,0:T(8,128)(2,1)}), bf16[128,80,128]{2,1,0:T(8,128)(2,1)S(1)}, u32[]{:S(2)}, u32[]{:S(2)}) %all-to-all-start.2) | async-done | bytes 2621472 | tf_op jit(solution)/shard_map/all_to_all | solution.py:495
  79.0 5.6 %all-to-all-start.1 = ((bf16[128,80,128]{2,1,0:T(8,128)(2,1)}), bf16[128,80,128]{2,1,0:T(8,128)(2,1)}, u32[]{:S(2)}, u32[]{:S(2)}) async-start(bf16[128,80,128]{2,1,0:T(8,128)(2,1)} %pack.3), calls=%async_computation.1 | async-start | bytes 5242880 | tf_op jit(solution)/shard_map/all_to_all | solution.py:495
  84.6 0.0 copy-done.9
  84.6 0.0 copy-start.2
  84.6 1.8 %copy-done.2 = bf16[33,48,512]{2,1,0:T(8,128)(2,1)S(1)} copy-done((bf16[33,48,512]{2,1,0:T(8,128)(2,1)S(1)}, bf16[33,48,512]{2,1,0:T(8,128)(2,1)}, u32[]{:S(2)}) %copy-start.2) | copy-done | bytes 1622040
  86.4 39.3 %near.1.old_hbm = f32[33,16,256]{2,1,0:T(8,128)S(1)} custom-call(s32[2,384]{1,0:T(2,128)S(1)} %get-tuple-element.28.list_ref, bf16[128,80,128]{2,1,0:T(8,128)(2,1)S(1)} %all-to-all-done.2.got_ref, bf16[33,48,512]{2,1,0:T(8,128)(2,1)S(1)} %copy-done.2, f32[33,16,256]{2,1,0:T(8,128)S(1)} %get-tuple-element.33.old_ref), custom_call_target="tpu_custom_call", output_to_operand_aliasing={{}: (3, {})} | custom-call | flops 335544320 | bytes 8388608 | tf_op jit(solution)/shard_map/near/pallas_call | solution.py:498
  125.7 0.8 copy-done.6
  126.5 5.4 %all-to-all-done.1.got_hbm = bf16[128,80,128]{2,1,0:T(8,128)(2,1)} async-done(((bf16[128,80,128]{2,1,0:T(8,128)(2,1)}), bf16[128,80,128]{2,1,0:T(8,128)(2,1)}, u32[]{:S(2)}, u32[]{:S(2)}) %all-to-all-start.1) | async-done | bytes 2621472 | tf_op jit(solution)/shard_map/all_to_all | solution.py:495
  131.9 16.0 %last.1 = bf16[16,8192]{1,0:T(8,128)(2,1)} custom-call(s32[2,384]{1,0:T(2,128)} %copy-done.9, s32[32,27]{1,0:T(8,128)} %multiply_add_fusion.code0_ref, s32[4,27]{1,0:T(4,128)} %add_add_fusion.code1_ref, bf16[128,80,128]{2,1,0:T(8,128)(2,1)} %all-to-all-done.1.got_hbm, bf16[33,48,512]{2,1,0:T(8,128)(2,1)} %copy-done, f32[33,16,256]{2,1,0:T(8,128)} %copy-done.6, ...), custom_call_target="tpu_custom_call" | custom-call | tf_op jit(solution)/shard_map/last/pallas_call | solution.py:514
  (5 shorter events, 0.1 us)
Async XLA Ops:
  6.5 16.6 %copy-start.5 = (bf16[16,8192]{1,0:T(8,128)(2,1)S(1)}, bf16[16,8192]{1,0:T(8,128)(2,1)}, u32[]{:S(2)}) copy-start(bf16[16,8192]{1,0:T(8,128)(2,1)} %x_ref.1) | copy-start | bytes 786436
  6.5 16.6 %copy-start.8 = (f32[8192]{0:T(1024)S(1)}, f32[8192]{0:T(1024)}, u32[]{:S(2)}) copy-start(f32[8192]{0:T(1024)} %param.15) | copy-start | bytes 98308
  6.5 125.3 %all-gather.2.cloned.1.call-start = ((), (), s32[]{:S(2)}) async-start(), calls=%async_computation.3 | async-start | bytes 9510912 | tf_op jit(solution)/shard_map/all_gather | solution.py:424
  9.7 21.1 %all-to-all-start = ((s32[128,1,128]{2,1,0:T(1,128)}), s32[128,1,128]{2,1,0:T(1,128)S(1)}, u32[]{:S(2)}, u32[]{:S(2)}) async-start(s32[128,1,128]{2,1,0:T(1,128)} %bitcast.20), calls=%async_computation | async-start | bytes 131072 | tf_op jit(solution)/shard_map/all_to_all | solution.py:425
  24.1 1.2 copy-start
  25.3 0.7 copy-start.3
  26.0 0.7 copy-start.7
  30.7 0.6 copy-start.11
  35.3 5.7 %copy-start.14 = (s32[4,27]{1,0:T(4,128)S(1)}, s32[4,27]{1,0:T(4,128)}, u32[]{:S(2)}) copy-start(s32[4,27]{1,0:T(4,128)} %param.23) | copy-start | bytes 1300
  35.3 5.8 %copy-start.15 = (s32[4,27]{1,0:T(4,128)S(1)}, s32[4,27]{1,0:T(4,128)}, u32[]{:S(2)}) copy-start(s32[4,27]{1,0:T(4,128)} %param.22) | copy-start | bytes 1300
  35.3 6.4 %copy-start.12 = (s32[32,27]{1,0:T(8,128)S(1)}, s32[32,27]{1,0:T(8,128)}, u32[]{:S(2)}) copy-start(s32[32,27]{1,0:T(8,128)} %param.21) | copy-start | bytes 10372
  35.3 6.4 %copy-start.13 = (s32[32,27]{1,0:T(8,128)S(1)}, s32[32,27]{1,0:T(8,128)}, u32[]{:S(2)}) copy-start(s32[32,27]{1,0:T(8,128)} %param.20) | copy-start | bytes 10372
  35.3 43.7 %all-to-all-start.2 = ((bf16[128,80,128]{2,1,0:T(8,128)(2,1)}), bf16[128,80,128]{2,1,0:T(8,128)(2,1)S(1)}, u32[]{:S(2)}, u32[]{:S(2)}) async-start(bf16[128,80,128]{2,1,0:T(8,128)(2,1)} %pack.2), calls=%async_computation.2 | async-start | bytes 5242880 | tf_op jit(solution)/shard_map/all_to_all | solution.py:495
  41.0 5.2 %copy-start.1 = (bf16[33,48,512]{2,1,0:T(8,128)(2,1)S(1)}, bf16[33,48,512]{2,1,0:T(8,128)(2,1)}, u32[]{:S(2)}) copy-start(bf16[33,48,512]{2,1,0:T(8,128)(2,1)} %copy-done) | copy-start | bytes 4866052
  41.0 5.2 %copy-start.4 = (bf16[16,80,128]{2,1,0:T(8,128)(2,1)S(1)}, bf16[16,80,128]{2,1,0:T(8,128)(2,1)}, u32[]{:S(2)}) copy-start(bf16[16,80,128]{2,1,0:T(8,128)(2,1)} %copy-done.3) | copy-start | bytes 983044
  41.0 5.1 %copy-start.10 = (s32[8,32]{1,0:T(8,128)S(1)}, s32[8,32]{1,0:T(8,128)}, u32[]{:S(2)}) copy-start(s32[8,32]{1,0:T(8,128)} %get-tuple-element.25.place_ref) | copy-start | bytes 3076
  55.0 29.5 %copy-start.9 = (s32[2,384]{1,0:T(2,128)}, s32[2,384]{1,0:T(2,128)S(1)}, u32[]{:S(2)}) copy-start(s32[2,384]{1,0:T(2,128)S(1)} %get-tuple-element.28.list_ref) | copy-start | bytes 9220
  79.0 52.9 %all-to-all-start.1 = ((bf16[128,80,128]{2,1,0:T(8,128)(2,1)}), bf16[128,80,128]{2,1,0:T(8,128)(2,1)}, u32[]{:S(2)}, u32[]{:S(2)}) async-start(bf16[128,80,128]{2,1,0:T(8,128)(2,1)} %pack.3), calls=%async_computation.1 | async-start | bytes 5242880 | tf_op jit(solution)/shard_map/all_to_all | solution.py:495
  84.6 1.8 %copy-start.2 = (bf16[33,48,512]{2,1,0:T(8,128)(2,1)S(1)}, bf16[33,48,512]{2,1,0:T(8,128)(2,1)}, u32[]{:S(2)}) copy-start(bf16[33,48,512]{2,1,0:T(8,128)(2,1)} %copy-done) | copy-start | bytes 4866052
  125.7 0.8 copy-start.6
Sparse Core Ops, SparseCore 0:
  10.5 119.2 all-gather.1

commit v6 on v5

--- a/solution.py
+++ b/solution.py
@@ -338,12 +338,10 @@
         (basis_hbm, basis_ref), (couple0_hbm, couple0_ref),
     ]
     copies = [pltpu.make_async_copy(a, b, sems.at[i]) for i, (a, b) in enumerate(pairs)]
-    for copy in copies[:3]:
+    for copy in copies:
         copy.start()
     for copy in copies[:3]:
         copy.wait()
-    for copy in copies[3:]:
-        copy.start()
     near_pairs(part, list_ref, got_ref, feature_ref, near_ref, square_ref, kernel_ref)
     for copy in copies[3:]:
         copy.wait()

time: 155 us -> 155 us (level)
  no operation moved by 1% of the time
where the time goes in v6:
time: 155 us; the launch traced here: 154 us
  Pallas kernels  75.2 us (49%)
  waiting for transfers between devices  33.4 us (22%)
  starting transfers between devices  22.8 us (15%)
  between operations  13.6 us (9%)
  local copies, waits for them, and re-layouts  7.74 us (5%)
    pallas_call x1, Pallas kernels, on_device(): pl.pallas_call(functools.partial(near_kernel, part), out_shape=total_shap...  39.3 us
    all_to_all x2, waiting for transfers between devices, on_device(): lax.all_to_all(packed[part], AXES, split_axis=0, concat_axis=0, tiled=True)  29.3 us
    pallas_call x1, Pallas kernels, on_device(): pl.pallas_call(functools.partial(last_kernel, parts - 1), out_shape=jax.S...  15.2 us
    all_to_all x1, starting transfers between devices, on_device(): lax.all_to_all(asked.reshape(devices, 1, devices), AXES, split_axis=0, co...  11.5 us
    all_to_all x2, starting transfers between devices, on_device(): lax.all_to_all(packed[part], AXES, split_axis=0, concat_axis=0, tiled=True)  11.3 us
    pallas_call x1, Pallas kernels, on_device(): pl.pallas_call(own_kernel, out_shape=(total_shape, jax.ShapeDtypeStruct((...  8.83 us
    pallas_call x2, Pallas kernels, pack(): pl.pallas_call(functools.partial(pack_kernel, part), out_shape=jax.ShapeD...  7.83 us
    unnamed x32, local copies, waits for them, and re-layouts  5.87 us
  transfers between devices with their start and end apart: 4, of which 3 were waited for; matrix products, arithmetic and copies ran while one was open for 2% of the time, Pallas kernels for 37%

profile of v6, /device:TPU:1, one launch (start us, length us, event | category | flops | bytes accessed | tf_op | source)
XLA Modules:
  0.0 154.0 jit_solution(10862875692157203736)
XLA Ops:
  6.5 0.0 copy-start.5
  6.5 0.0 copy-start.8
  6.5 0.0 all-gather.2.cloned.1.call-start
  6.5 3.1 %first.1 = (bf16[18,16,128]{2,1,0:T(8,128)(2,1)}, s32[128,128]{1,0:T(8,128)}, s32[8,32]{1,0:T(8,128)}) custom-call(bf16[16,8192]{1,0:T(8,128)(2,1)} %x_ref.1, bf16[32,64,256]{2,1,0:T(8,128)(2,1)} %basis_hbm.3, bf16[4,64,512]{2,1,0:T(8,128)(2,1)} %transfer_hbm.3, s32[8,32]{1,0:T(8,128)} %bitcast.21, s32[8,32]{1,0:T(8,128)} %bitcast.22), custom_call_target="tpu_custom_call" | custom-call | tf_op jit(solution)/shard_map/first/pallas_call | solution.py:402
  9.6 0.0 all-gather.2.cloned.1.call-update
  9.7 11.5 %all-to-all-start = ((s32[128,1,128]{2,1,0:T(1,128)}), s32[128,1,128]{2,1,0:T(1,128)S(1)}, u32[]{:S(2)}, u32[]{:S(2)}) async-start(s32[128,1,128]{2,1,0:T(1,128)} %bitcast.20), calls=%async_computation | async-start | bytes 131072 | tf_op jit(solution)/shard_map/all_to_all | solution.py:423
  21.2 0.9 pad.8
  22.1 0.9 pad_bitcast_fusion
  23.1 0.0 copy-done.5
  23.1 0.0 copy-done.8
  23.1 1.0 prepare.1
  24.1 0.0 copy-start
  24.1 1.2 copy-done
  25.3 0.0 copy-start.3
  25.3 0.7 copy-done.3
  26.0 0.0 copy-start.7
  26.0 0.7 copy-done.7
  26.7 4.1 %all-to-all-done = s32[128,1,128]{2,1,0:T(1,128)S(1)} async-done(((s32[128,1,128]{2,1,0:T(1,128)}), s32[128,1,128]{2,1,0:T(1,128)S(1)}, u32[]{:S(2)}, u32[]{:S(2)}) %all-to-all-start) | async-done | bytes 65568 | tf_op jit(solution)/shard_map/all_to_all | solution.py:423
  30.7 0.0 copy-start.11
  30.7 0.6 copy-done.11
  31.4 3.9 %pack.2 = bf16[128,80,128]{2,1,0:T(8,128)(2,1)} custom-call(s32[128,128]{1,0:T(8,128)} %bitcast.16, bf16[16,80,128]{2,1,0:T(8,128)(2,1)} %copy-done.3, f32[32,8,128]{2,1,0:T(8,128)} %copy-done.7), custom_call_target="tpu_custom_call" | custom-call | tf_op jit(solution)/shard_map/pack/pallas_call | solution.py:455
  35.3 0.0 copy-start.14
  35.3 0.0 copy-start.13
  35.3 5.7 %all-to-all-start.2 = ((bf16[128,80,128]{2,1,0:T(8,128)(2,1)}), bf16[128,80,128]{2,1,0:T(8,128)(2,1)S(1)}, u32[]{:S(2)}, u32[]{:S(2)}) async-start(bf16[128,80,128]{2,1,0:T(8,128)(2,1)} %pack.2), calls=%async_computation.2 | async-start | bytes 5242880 | tf_op jit(solution)/shard_map/all_to_all | solution.py:493
  41.0 0.0 copy-done.14
  41.0 0.0 copy-done.15
  41.0 0.0 copy-start.1
  41.0 0.0 copy-start.4
  41.0 0.0 copy-start.10
  41.1 0.6 add_add_fusion.code1_ref
  41.6 0.0 copy-done.12
  41.6 0.0 copy-done.13
  41.6 0.6 multiply_add_fusion.code0_ref
  42.3 3.9 %pack.3 = bf16[128,80,128]{2,1,0:T(8,128)(2,1)} custom-call(s32[128,128]{1,0:T(8,128)} %bitcast.17, bf16[16,80,128]{2,1,0:T(8,128)(2,1)} %copy-done.3, f32[32,8,128]{2,1,0:T(8,128)} %copy-done.7), custom_call_target="tpu_custom_call" | custom-call | tf_op jit(solution)/shard_map/pack/pallas_call | solution.py:455
  46.2 0.0 copy-done.1
  46.2 0.0 copy-done.4
  46.2 0.0 copy-done.10
  46.2 8.8 %own.1 = (f32[33,16,256]{2,1,0:T(8,128)S(1)}, s32[2,384]{1,0:T(2,128)S(1)}) custom-call(s32[8,32]{1,0:T(8,128)S(1)} %copy-done.10, bf16[16,80,128]{2,1,0:T(8,128)(2,1)S(1)} %copy-done.4, bf16[33,48,512]{2,1,0:T(8,128)(2,1)S(1)} %copy-done.1), custom_call_target="tpu_custom_call" | custom-call | flops 83886080 | bytes 4194304 | tf_op jit(solution)/shard_map/own/pallas_call | solution.py:473
  55.0 0.0 copy-start.9
  55.0 24.0 %all-to-all-done.2.got_ref = bf16[128,80,128]{2,1,0:T(8,128)(2,1)S(1)} async-done(((bf16[128,80,128]{2,1,0:T(8,128)(2,1)}), bf16[128,80,128]{2,1,0:T(8,128)(2,1)S(1)}, u32[]{:S(2)}, u32[]{:S(2)}) %all-to-all-start.2) | async-done | bytes 2621472 | tf_op jit(solution)/shard_map/all_to_all | solution.py:493
  79.0 5.6 %all-to-all-start.1 = ((bf16[128,80,128]{2,1,0:T(8,128)(2,1)}), bf16[128,80,128]{2,1,0:T(8,128)(2,1)}, u32[]{:S(2)}, u32[]{:S(2)}) async-start(bf16[128,80,128]{2,1,0:T(8,128)(2,1)} %pack.3), calls=%async_computation.1 | async-start | bytes 5242880 | tf_op jit(solution)/shard_map/all_to_all | solution.py:493
  84.6 0.0 copy-done.9
  84.6 0.0 copy-start.2
  84.6 1.8 %copy-done.2 = bf16[33,48,512]{2,1,0:T(8,128)(2,1)S(1)} copy-done((bf16[33,48,512]{2,1,0:T(8,128)(2,1)S(1)}, bf16[33,48,512]{2,1,0:T(8,128)(2,1)}, u32[]{:S(2)}) %copy-start.2) | copy-done | bytes 1622040
  86.4 39.3 %near.1.old_hbm = f32[33,16,256]{2,1,0:T(8,128)S(1)} custom-call(s32[2,384]{1,0:T(2,128)S(1)} %get-tuple-element.28.list_ref, bf16[128,80,128]{2,1,0:T(8,128)(2,1)S(1)} %all-to-all-done.2.got_ref, bf16[33,48,512]{2,1,0:T(8,128)(2,1)S(1)} %copy-done.2, f32[33,16,256]{2,1,0:T(8,128)S(1)} %get-tuple-element.33.old_ref), custom_call_target="tpu_custom_call", output_to_operand_aliasing={{}: (3, {})} | custom-call | flops 335544320 | bytes 8388608 | tf_op jit(solution)/shard_map/near/pallas_call | solution.py:496
  125.7 0.8 copy-done.6
  126.5 5.4 %all-to-all-done.1.got_hbm = bf16[128,80,128]{2,1,0:T(8,128)(2,1)} async-done(((bf16[128,80,128]{2,1,0:T(8,128)(2,1)}), bf16[128,80,128]{2,1,0:T(8,128)(2,1)}, u32[]{:S(2)}, u32[]{:S(2)}) %all-to-all-start.1) | async-done | bytes 2621472 | tf_op jit(solution)/shard_map/all_to_all | solution.py:493
  131.9 15.2 %last.1 = bf16[16,8192]{1,0:T(8,128)(2,1)} custom-call(s32[2,384]{1,0:T(2,128)} %copy-done.9, s32[32,27]{1,0:T(8,128)} %multiply_add_fusion.code0_ref, s32[4,27]{1,0:T(4,128)} %add_add_fusion.code1_ref, bf16[128,80,128]{2,1,0:T(8,128)(2,1)} %all-to-all-done.1.got_hbm, bf16[33,48,512]{2,1,0:T(8,128)(2,1)} %copy-done, f32[33,16,256]{2,1,0:T(8,128)} %copy-done.6, ...), custom_call_target="tpu_custom_call" | custom-call | tf_op jit(solution)/shard_map/last/pallas_call | solution.py:512
  (5 shorter events, 0.1 us)
Async XLA Ops:
  6.5 16.6 %copy-start.5 = (bf16[16,8192]{1,0:T(8,128)(2,1)S(1)}, bf16[16,8192]{1,0:T(8,128)(2,1)}, u32[]{:S(2)}) copy-start(bf16[16,8192]{1,0:T(8,128)(2,1)} %x_ref.1) | copy-start | bytes 786436
  6.5 16.6 %copy-start.8 = (f32[8192]{0:T(1024)S(1)}, f32[8192]{0:T(1024)}, u32[]{:S(2)}) copy-start(f32[8192]{0:T(1024)} %param.15) | copy-start | bytes 98308
  6.5 125.3 %all-gather.2.cloned.1.call-start = ((), (), s32[]{:S(2)}) async-start(), calls=%async_computation.3 | async-start | bytes 9510912 | tf_op jit(solution)/shard_map/all_gather | solution.py:422
  9.7 21.1 %all-to-all-start = ((s32[128,1,128]{2,1,0:T(1,128)}), s32[128,1,128]{2,1,0:T(1,128)S(1)}, u32[]{:S(2)}, u32[]{:S(2)}) async-start(s32[128,1,128]{2,1,0:T(1,128)} %bitcast.20), calls=%async_computation | async-start | bytes 131072 | tf_op jit(solution)/shard_map/all_to_all | solution.py:423
  24.1 1.2 copy-start
  25.3 0.7 copy-start.3
  26.0 0.7 copy-start.7
  30.7 0.6 copy-start.11
  35.3 5.7 %copy-start.14 = (s32[4,27]{1,0:T(4,128)S(1)}, s32[4,27]{1,0:T(4,128)}, u32[]{:S(2)}) copy-start(s32[4,27]{1,0:T(4,128)} %param.23) | copy-start | bytes 1300
  35.3 5.8 %copy-start.15 = (s32[4,27]{1,0:T(4,128)S(1)}, s32[4,27]{1,0:T(4,128)}, u32[]{:S(2)}) copy-start(s32[4,27]{1,0:T(4,128)} %param.22) | copy-start | bytes 1300
  35.3 6.4 %copy-start.12 = (s32[32,27]{1,0:T(8,128)S(1)}, s32[32,27]{1,0:T(8,128)}, u32[]{:S(2)}) copy-start(s32[32,27]{1,0:T(8,128)} %param.21) | copy-start | bytes 10372
  35.3 6.4 %copy-start.13 = (s32[32,27]{1,0:T(8,128)S(1)}, s32[32,27]{1,0:T(8,128)}, u32[]{:S(2)}) copy-start(s32[32,27]{1,0:T(8,128)} %param.20) | copy-start | bytes 10372
  35.3 43.7 %all-to-all-start.2 = ((bf16[128,80,128]{2,1,0:T(8,128)(2,1)}), bf16[128,80,128]{2,1,0:T(8,128)(2,1)S(1)}, u32[]{:S(2)}, u32[]{:S(2)}) async-start(bf16[128,80,128]{2,1,0:T(8,128)(2,1)} %pack.2), calls=%async_computation.2 | async-start | bytes 5242880 | tf_op jit(solution)/shard_map/all_to_all | solution.py:493
  41.0 5.2 %copy-start.1 = (bf16[33,48,512]{2,1,0:T(8,128)(2,1)S(1)}, bf16[33,48,512]{2,1,0:T(8,128)(2,1)}, u32[]{:S(2)}) copy-start(bf16[33,48,512]{2,1,0:T(8,128)(2,1)} %copy-done) | copy-start | bytes 4866052
  41.0 5.2 %copy-start.4 = (bf16[16,80,128]{2,1,0:T(8,128)(2,1)S(1)}, bf16[16,80,128]{2,1,0:T(8,128)(2,1)}, u32[]{:S(2)}) copy-start(bf16[16,80,128]{2,1,0:T(8,128)(2,1)} %copy-done.3) | copy-start | bytes 983044
  41.0 5.1 %copy-start.10 = (s32[8,32]{1,0:T(8,128)S(1)}, s32[8,32]{1,0:T(8,128)}, u32[]{:S(2)}) copy-start(s32[8,32]{1,0:T(8,128)} %get-tuple-element.25.place_ref) | copy-start | bytes 3076
  55.0 29.5 %copy-start.9 = (s32[2,384]{1,0:T(2,128)}, s32[2,384]{1,0:T(2,128)S(1)}, u32[]{:S(2)}) copy-start(s32[2,384]{1,0:T(2,128)S(1)} %get-tuple-element.28.list_ref) | copy-start | bytes 9220
  79.0 52.9 %all-to-all-start.1 = ((bf16[128,80,128]{2,1,0:T(8,128)(2,1)}), bf16[128,80,128]{2,1,0:T(8,128)(2,1)}, u32[]{:S(2)}, u32[]{:S(2)}) async-start(bf16[128,80,128]{2,1,0:T(8,128)(2,1)} %pack.3), calls=%async_computation.1 | async-start | bytes 5242880 | tf_op jit(solution)/shard_map/all_to_all | solution.py:493
  84.6 1.8 %copy-start.2 = (bf16[33,48,512]{2,1,0:T(8,128)(2,1)S(1)}, bf16[33,48,512]{2,1,0:T(8,128)(2,1)}, u32[]{:S(2)}) copy-start(bf16[33,48,512]{2,1,0:T(8,128)(2,1)} %copy-done) | copy-start | bytes 4866052
  125.7 0.8 copy-start.6
Sparse Core Ops, SparseCore 0:
  10.5 119.2 all-gather.1
